TPU v7x, 32 devices: a whole 2x2x4 slice. The times are simulated.
32 devices in a mesh: grp: 2 (over y), section: 2 (over x), lat: 2 (over core), lon: 4 (over z).
Axes of the slice: x: 2, y: 2, z: 4, core: 2. Of those that a mesh axis runs over, the one named last changes fastest.
Arguments:
- section_input: bfloat16 [2, 64, 32, 1536], P('section', ('grp', 'lat'), 'lon'), parts along dimension 1, may hold values from -6 to 6
- fresh_input: bfloat16 [64, 32, 1536], P(('grp', 'lat'), 'lon'), parts along dimension 0, may hold values from -6 to 6
- offsets: int32 [4], P('grp'), parts along dimension 0, may hold values from 1 to 4, as said below
- regions: int32 [64, 32], P(('grp', 'lat'), 'lon'), parts along dimension 0, may hold values from 0 to 8, as said below
- up_weight: bfloat16 [2, 1536, 3072], P('section', 'lon', 'lat'), may hold values from -0.15625 to 0.15625
- up_bias: float32 [2, 3072], P('section', 'lat'), may hold values from -3 to 3
- down_weight: bfloat16 [2, 3072, 1536], P('section', 'lat', 'lon'), may hold values from -0.109375 to 0.109375
- mlp_gain: float32 [2, 1536], P('section'), may hold values from 0.5 to 1.5
- qkv_weight: bfloat16 [2, 1536, 3, 768], P('section', 'lon', None, 'lat'), may hold values from -0.15625 to 0.15625
- logit_scale: float32 [2, 12], P('section', 'lat'), may hold values from 2 to 20
- position_bias: float32 [2, 12, 64, 64], P('section', 'lat'), may hold values from 0 to 8
- out_weight: bfloat16 [2, 768, 1536], P('section', 'lat', 'lon'), may hold values from -0.21875 to 0.21875
- attn_gain: float32 [2, 1536], P('section'), may hold values from 0.5 to 1.5
Outputs:
- handed: bfloat16 [2, 64, 32, 1536], P('section', ('grp', 'lat'), 'lon'), parts along dimension 1
- opened: bfloat16 [2, 64, 32, 1536], P('section', ('grp', 'lat'), 'lon'), parts along dimension 1
There are 2 independent parts, one for each index of `grp`. A program takes and returns all parts, laid end to end along the dimension named above; an argument that names none is the same for every part. Nothing has to cross between parts.
Inputs may be any that keep to these rules, and one draw needn't show every extreme that they name: offsets[0] is the latitude shift and offsets[1] the longitude shift; at least one of them equals 4. `regions`: the shifted-window region id of each token of the rolled grid: 3 * a + b, where a is 0 for rows i < 24, 1 for 24 <= i < 32 - offsets[0] and 2 for the rest, and b is the same for columns with 32 and offsets[1].
All inputs are finite; a program needn't handle non-finite values.
Results may differ from a plain program's by a relative error of at most 0.014.
Values may be sent and summed in bfloat16 or wider, within the bound.
A program may use at most 64 MiB of HBM per device.

v0:
```python
import jax
import jax.numpy as jnp
from jax import lax
from jax.sharding import PartitionSpec as P

W = 8


def shifted(array, axis, by):
    count = lax.axis_size(axis)
    pairs = [(i, i + by) for i in range(count) if 0 <= i + by < count]
    return lax.ppermute(array, axis, pairs)


def from_behind(block, axis, distance):
    devices = range(lax.axis_size(axis))
    route = [((i - distance) % len(devices), i) for i in devices]
    return lax.ppermute(block, axis, route)


def layer_norm(total, norm_gain):
    mean = jnp.mean(total, axis=-1, keepdims=True)
    centered = total - mean
    variance = jnp.mean(centered * centered, axis=-1, keepdims=True)
    return centered * lax.rsqrt(variance + 1e-05) * norm_gain


def windows(values, side):
    height, breadth = (values.shape[0], values.shape[1])
    rest = values.shape[2:]
    blocks = values.reshape((height // side, side, breadth // side, side) + rest)
    blocks = jnp.moveaxis(blocks, 2, 1)
    return blocks.reshape((-1, side * side) + rest)


def unwindow(values, height, breadth, side):
    rest = values.shape[2:]
    blocks = values.reshape((height // side, breadth // side, side, side) + rest)
    blocks = jnp.moveaxis(blocks, 1, 2)
    return blocks.reshape((height, breadth) + rest)


def attend(packed, region_marks, head_scale, pos_bias):
    blocks = windows(packed, W)
    query_rows = blocks[:, :, 0]
    key_rows = blocks[:, :, 1]
    value_rows = blocks[:, :, 2]
    inner_dot = jnp.einsum(
        "wihd,wjhd->whij", query_rows, key_rows, preferred_element_type=jnp.float32
    )
    query_wide = query_rows.astype(jnp.float32)
    key_wide = key_rows.astype(jnp.float32)
    query_norm = lax.rsqrt(jnp.sum(query_wide * query_wide, axis=-1) + 1e-06)
    key_norm = lax.rsqrt(jnp.sum(key_wide * key_wide, axis=-1) + 1e-06)
    cosine = inner_dot * jnp.transpose(query_norm, (0, 2, 1))[:, :, :, None]
    cosine = cosine * jnp.transpose(key_norm, (0, 2, 1))[:, :, None, :]
    score = cosine * head_scale[None, :, None, None] + pos_bias[None]
    marked = windows(region_marks, W)
    same_region = (marked[:, :, None] == marked[:, None, :])[:, None]
    raw_weights = jnp.where(same_region, jnp.exp(score), jnp.float32(0.0))
    weights = (raw_weights / jnp.sum(raw_weights, axis=-1, keepdims=True)).astype(jnp.bfloat16)
    context = jnp.einsum("whij,wjhd->wihd", weights, value_rows, preferred_element_type=jnp.float32)
    return context.astype(jnp.bfloat16)


def per_device(
    section_input,
    fresh_input,
    offsets,
    regions,
    up_weight,
    up_bias,
    down_weight,
    mlp_gain,
    qkv_weight,
    logit_scale,
    position_bias,
    out_weight,
    attn_gain,
):
    tile_in = section_input[0]
    height, breadth, width = tile_in.shape
    gathered = lax.all_gather(tile_in, "lat", axis=0, tiled=True)
    flat_rows = gathered.reshape(-1, width)
    up_local = up_weight[0]
    columns = flat_rows
    pre_act = jnp.dot(
        columns,
        lax.all_gather(up_local, "lon", axis=0, tiled=True),
        preferred_element_type=jnp.float32,
    )
    hidden = jax.nn.gelu(pre_act + up_bias[0], approximate=False).astype(jnp.bfloat16)
    down_terms = jnp.dot(
        hidden,
        lax.all_gather(down_weight[0], "lon", axis=1, tiled=True),
        preferred_element_type=jnp.float32,
    )
    mlp_sum = lax.psum_scatter(
        down_terms.astype(jnp.bfloat16), "lat", scatter_dimension=0, tiled=True
    ).astype(jnp.float32)
    handed_flat = tile_in.reshape(-1, width).astype(jnp.float32) + layer_norm(mlp_sum, mlp_gain[0])
    handed = handed_flat.astype(jnp.bfloat16).reshape(height, breadth, width)
    passed = shifted(handed, "section", 1)
    first_section = lax.axis_index("section") == 0
    entering = jnp.where(first_section, fresh_input, passed)
    shift_lat = offsets[0]
    shift_lon = offsets[1]
    strip_width = W // 2
    after_strip = from_behind(entering[:, :strip_width], "lon", -1)
    rolled = lax.dynamic_slice_in_dim(
        jnp.concatenate([entering, after_strip], 1), shift_lon, breadth, 1
    )
    region_marks = regions.astype(jnp.bfloat16)
    grid, grid_marks = (
        lax.all_gather(rolled, "lat", axis=0, tiled=True),
        lax.all_gather(region_marks, "lat", axis=0, tiled=True),
    )
    grid = jnp.roll(grid, -shift_lat, axis=0)
    grid_height = grid.shape[0]
    flat_grid = grid.reshape(-1, width)
    heads_local = logit_scale.shape[1]
    head_size = qkv_weight.shape[3] // heads_local
    piece = lax.all_gather(qkv_weight[0], "lon", axis=0, tiled=True)
    columns = flat_grid
    packed = jnp.dot(columns, piece.reshape(piece.shape[0], -1), preferred_element_type=jnp.float32)
    packed = packed.astype(jnp.bfloat16).reshape(grid_height, breadth, 3, heads_local, head_size)
    context = attend(packed, grid_marks, logit_scale[0], position_bias[0])
    context = unwindow(context, grid_height, breadth, W).reshape(
        grid_height * breadth, heads_local * head_size
    )
    out_terms = jnp.dot(
        context,
        lax.all_gather(out_weight[0], "lon", axis=1, tiled=True),
        preferred_element_type=jnp.float32,
    )
    out_terms = jnp.roll(out_terms.reshape(grid_height, breadth, width), shift_lat, axis=0).reshape(
        -1, width
    )
    attn_sum = lax.psum_scatter(
        out_terms.astype(jnp.bfloat16), "lat", scatter_dimension=0, tiled=True
    ).astype(jnp.float32)
    branch = layer_norm(attn_sum, attn_gain[0]).astype(jnp.bfloat16).reshape(height, breadth, width)
    tail_strip = from_behind(branch[:, -strip_width:], "lon", 1)
    branch = lax.dynamic_slice_in_dim(
        jnp.concatenate([tail_strip, branch], 1), strip_width - shift_lon, breadth, 1
    )
    opened = (entering.astype(jnp.float32) + branch.astype(jnp.float32)).astype(jnp.bfloat16)
    return (handed[None], opened[None])


def solution(mesh):
    return jax.shard_map(
        per_device,
        mesh=mesh,
        in_specs=(
            P("section", ("grp", "lat"), "lon", None),
            P(("grp", "lat"), "lon", None),
            P("grp"),
            P(("grp", "lat"), "lon"),
            P("section", "lon", "lat"),
            P("section", "lat"),
            P("section", "lat", "lon"),
            P("section", None),
            P("section", "lon", None, "lat"),
            P("section", "lat"),
            P("section", "lat", None, None),
            P("section", "lat", "lon"),
            P("section", None),
        ),
        out_specs=(
            P("section", ("grp", "lat"), "lon", None),
            P("section", ("grp", "lat"), "lon", None),
        ),
        check_vma=False,
    )
```

profile of v0, /device:TPU:0, one launch (start us, length us, event | category | flops | bytes accessed | tf_op | source)
XLA Modules:
  0.0 347.0 jit_solution(9422271681965755356)
XLA Ops:
  8.8 2.4 all-gather
  11.2 90.5 %all-gather.11.cloned.1.call-done = bf16[1,1536,1536]{2,1,0:T(8,128)(2,1)} async-done(((bf16[1,384,1536]{2,1,0:T(8,128)(2,1)}), bf16[1,1536,1536]{2,1,0:T(8,128)(2,1)}) %all-gather.11.cloned.1.call-update) | async-done | bytes 4718608 | tf_op jit(solution)/shard_map/all_gather | solution.py:89
  101.7 89.4 %all-gather.13.cloned.1.call-done = bf16[1,1536,1536]{2,1,0:T(8,128)(2,1)} async-done(((bf16[1,1536,384]{2,1,0:T(8,128)(2,1)}), bf16[1,1536,1536]{2,1,0:T(8,128)(2,1)}) %all-gather.13.cloned.1.call-update) | async-done | bytes 4718608 | tf_op jit(solution)/shard_map/all_gather | solution.py:95
  191.2 10.1 %fusion.7 = bf16[256,1536]{1,0:T(8,128)(2,1)} fusion(bf16[1,1536,1536]{2,1,0:T(8,128)(2,1)} %all-gather.13.cloned.1.call-done, bf16[1,1536,1536]{2,1,0:T(8,128)(2,1)} %all-gather.11.cloned.1.call-done, bf16[1,32,8,1536]{3,2,0,1:T(8,128)(2,1)S(1)} %all-gather, f32[1536]{0:T(1024)S(1)} %reduce), kind=kOutput, calls=%fused_computation.8 | convolution fusion | flops 2442264576 | bytes 11016192 | tf_op jit(solution)/shard_map/dot_general | solution.py:93
  201.4 2.2 copy.30
  203.7 4.6 %reduce-scatter.3.cloned.1.call-done = bf16[128,1536]{1,0:T(8,128)(2,1)} async-done(((bf16[256,1536]{1,0:T(8,128)(2,1)}), bf16[128,1536]{1,0:T(8,128)(2,1)}) %reduce-scatter.3.cloned.1.call-update) | async-done | bytes 393232 | tf_op jit(solution)/shard_map/reduce_scatter | solution.py:98
  208.2 1.1 convert_reduce_fusion.1
  209.3 1.2 fusion.41
  210.6 1.3 fusion.128
  211.9 3.6 %collective-permute-start = (bf16[16,8,1536]{2,1,0:T(8,128)(2,1)S(1)}, bf16[16,8,1536]{2,1,0:T(8,128)(2,1)S(1)}, u32[]{:S(2)}, u32[]{:S(2)}) collective-permute-start(bf16[16,8,1536]{2,1,0:T(8,128)(2,1)S(1)} %fusion.128), channel_id=1, source_target_pairs={{0,8},{1,9},{2,10},{3,11},{4,12},{5,13},{6,14},{7,15},{16,24},{17,... | collective-permute-start | bytes 1179656 | tf_op jit(solution)/shard_map/ppermute | solution.py:12
  220.9 1.8 all-gather.5
  224.5 3.4 collective-permute-start.1
  228.6 13.0 %collective-permute-done.1 = bf16[16,4,1536]{2,1,0:T(4,128)(2,1)S(1)} collective-permute-done((bf16[16,4,1536]{2,1,0:T(4,128)(2,1)S(1)}, bf16[16,4,1536]{2,1,0:T(4,128)(2,1)S(1)}, u32[]{:S(2)}, u32[]{:S(2)}) %collective-permute-start.1) | collective-permute-done | bytes 196640 | tf_op jit(solution)/shard_map/ppermute | solution.py:18
  242.0 2.5 all_gather.24
  244.5 40.4 %all-gather.15.cloned.1.call-done = bf16[1,1536,3,384]{1,3,2,0:T(8,128)(2,1)} async-done(((bf16[1,384,3,384]{1,3,2,0:T(8,128)(2,1)}), bf16[1,1536,3,384]{1,3,2,0:T(8,128)(2,1)}) %all-gather.15.cloned.1.call-update) | async-done | bytes 3538960 | tf_op jit(solution)/shard_map/all_gather | solution.py:123
  285.0 3.4 convolution_convert_fusion
  292.2 23.2 %all-gather.17.cloned.1.call-done = bf16[1,384,1536]{2,1,0:T(8,128)(2,1)} async-done(((bf16[1,384,384]{2,1,0:T(8,128)(2,1)}), bf16[1,384,1536]{2,1,0:T(8,128)(2,1)}) %all-gather.17.cloned.1.call-update) | async-done | bytes 1179664 | tf_op jit(solution)/shard_map/all_gather | solution.py:133
  315.4 1.8 fusion.30
  317.2 1.2 fusion.48
  319.8 6.5 %reduce-scatter.5.cloned.1.call-done = bf16[128,1536]{1,0:T(8,128)(2,1)} async-done(((bf16[256,1536]{1,0:T(8,128)(2,1)}), bf16[128,1536]{1,0:T(8,128)(2,1)}) %reduce-scatter.5.cloned.1.call-update) | async-done | bytes 393232 | tf_op jit(solution)/shard_map/reduce_scatter | solution.py:139
  327.4 1.2 fusion.38
  328.7 1.3 fusion.85
  330.1 1.8 collective-permute-start.2
  332.9 6.2 %collective-permute-done.2 = bf16[16,4,1536]{2,1,0:T(4,128)(2,1)S(1)} collective-permute-done((bf16[16,4,1536]{2,1,0:T(4,128)(2,1)S(1)}, bf16[16,4,1536]{2,1,0:T(4,128)(2,1)S(1)}, u32[]{:S(2)}, u32[]{:S(2)}) %collective-permute-start.2) | collective-permute-done | bytes 196640 | tf_op jit(solution)/shard_map/ppermute | solution.py:18
  (71 shorter events, 12.5 us)
Async XLA Ops:
  7.2 1.6 copy-start.7
  7.2 1.6 copy-start.1
  7.2 94.5 %all-gather.11.cloned.1.call-start = ((), (), s32[]{:S(2)}) async-start(), calls=%async_computation.4 | async-start | bytes 5898240 | tf_op jit(solution)/shard_map/all_gather | solution.py:89
  7.9 183.3 %all-gather.13.cloned.1.call-start = ((), (), s32[]{:S(2)}) async-start(), calls=%async_computation.5 | async-start | bytes 5898240 | tf_op jit(solution)/shard_map/all_gather | solution.py:95
  8.7 199.5 %reduce-scatter.3.cloned.1.call-start = ((), (), s32[]{:S(2)}) async-start(), calls=%async_computation.2 | async-start | bytes 1179648 | tf_op jit(solution)/shard_map/reduce_scatter | solution.py:98
  11.2 190.1 %copy-start.2 = (bf16[1,384,3,384]{3,1,2,0:T(8,128)(2,1)S(1)}, bf16[1,384,3,384]{3,1,2,0:T(8,128)(2,1)}, u32[]{:S(2)}) copy-start(bf16[1,384,3,384]{3,1,2,0:T(8,128)(2,1)} %param.21) | copy-start | bytes 2654212
  201.3 2.3 copy-start.8
  201.3 83.7 %all-gather.15.cloned.1.call-start = ((), (), s32[]{:S(2)}) async-start(), calls=%async_computation.6 | async-start | bytes 4423680 | tf_op jit(solution)/shard_map/all_gather | solution.py:123
  203.5 12.1 %copy-start.11 = (s32[2]{0:T(128)S(1)}, s32[2]{0:T(128)}, u32[]{:S(2)}) copy-start(s32[2]{0:T(128)} %param.15) | copy-start | bytes 28
  203.5 16.6 %copy-start.4 = (f32[1,6,64,64]{3,2,1,0:T(8,128)S(1)}, f32[1,6,64,64]{3,2,1,0:T(8,128)}, u32[]{:S(2)}) copy-start(f32[1,6,64,64]{3,2,1,0:T(8,128)} %param.23) | copy-start | bytes 294916
  203.5 17.4 %copy-start.10 = (s32[16,8]{0,1:T(8,128)S(1)}, s32[16,8]{0,1:T(8,128)}, u32[]{:S(2)}) copy-start(s32[16,8]{0,1:T(8,128)} %param.16) | copy-start | bytes 1540
  203.6 20.8 %copy-start.3 = (bf16[16,8,1536]{2,1,0:T(8,128)(2,1)S(1)}, bf16[16,8,1536]{2,1,0:T(8,128)(2,1)}, u32[]{:S(2)}) copy-start(bf16[16,8,1536]{2,1,0:T(8,128)(2,1)} %param.14) | copy-start | bytes 1179652
  203.6 111.8 %all-gather.17.cloned.1.call-start = ((), (), s32[]{:S(2)}) async-start(), calls=%async_computation.7 | async-start | bytes 1474560 | tf_op jit(solution)/shard_map/all_gather | solution.py:133
  211.9 12.4 %collective-permute-start = (bf16[16,8,1536]{2,1,0:T(8,128)(2,1)S(1)}, bf16[16,8,1536]{2,1,0:T(8,128)(2,1)S(1)}, u32[]{:S(2)}, u32[]{:S(2)}) collective-permute-start(bf16[16,8,1536]{2,1,0:T(8,128)(2,1)S(1)} %fusion.128), channel_id=1, source_target_pairs={{0,8},{1,9},{2,10},{3,11},{4,12},{5,13},{6,14},{7,15},{16,24},{17,... | collective-permute-start | bytes 1179656 | tf_op jit(solution)/shard_map/ppermute | solution.py:12
  215.6 110.7 %reduce-scatter.5.cloned.1.call-start = ((), (), s32[]{:S(2)}) async-start(), calls=%async_computation.3 | async-start | bytes 1179648 | tf_op jit(solution)/shard_map/reduce_scatter | solution.py:139
  224.5 17.2 %collective-permute-start.1 = (bf16[16,4,1536]{2,1,0:T(4,128)(2,1)S(1)}, bf16[16,4,1536]{2,1,0:T(4,128)(2,1)S(1)}, u32[]{:S(2)}, u32[]{:S(2)}) collective-permute-start(bf16[16,4,1536]{2,1,0:T(4,128)(2,1)S(1)} %slice.28), channel_id=1, source_target_pairs={{1,0},{2,1},{3,2},{0,3},{5,4},{6,5},{7,6},{4,7},{9,8},{10,9},{11,1... | collective-permute-start | bytes 589832 | tf_op jit(solution)/shard_map/ppermute | solution.py:18
  289.6 1.2 copy-start.5
  289.6 1.2 copy-start.6
  289.6 1.2 copy-start.12
  317.2 1.2 copy-start.9
  318.4 13.4 %copy-start = (bf16[128,1536]{1,0:T(8,128)(2,1)S(1)}, bf16[128,1536]{1,0:T(8,128)(2,1)}, u32[]{:S(2)}) copy-start(bf16[128,1536]{1,0:T(8,128)(2,1)} %reduce-scatter.3.cloned.1.call-done) | copy-start | bytes 1179652
  330.1 9.0 %collective-permute-start.2 = (bf16[16,4,1536]{2,1,0:T(4,128)(2,1)S(1)}, bf16[16,4,1536]{2,1,0:T(4,128)(2,1)S(1)}, u32[]{:S(2)}, u32[]{:S(2)}) collective-permute-start(bf16[16,4,1536]{2,1,0:T(4,128)(2,1)S(1)} %slice.32), channel_id=1, source_target_pairs={{3,0},{0,1},{1,2},{2,3},{7,4},{4,5},{5,6},{6,7},{11,8},{8,9},{9,10... | collective-permute-start | bytes 589832 | tf_op jit(solution)/shard_map/ppermute | solution.py:18
Sparse Core Ops, SparseCore 0:
  9.6 92.0 all-gather.10
  103.3 87.8 all-gather.12
  201.4 6.7 reduce-scatter.2
  209.7 75.1 all-gather.14
  286.5 28.8 all-gather.16
  318.5 7.6 reduce-scatter.4
where the time goes:
time: 348 us; the launch traced here: 347 us
  waiting for transfers between devices  276 us (79%)
  between operations  20.2 us (6%)
  matrix products  16 us (5%)
  other arithmetic  12.5 us (4%)
  starting transfers between devices  9.02 us (3%)
  blocking collectives  6.77 us (2%)
  local copies, waits for them, and re-layouts  6.41 us (2%)
    all_gather x1, waiting for transfers between devices, per_device(): lax.all_gather(up_local, 'lon', axis=0, tiled=True)  90.5 us
    all_gather x1, waiting for transfers between devices, per_device(): lax.all_gather(down_weight[0], 'lon', axis=1, tiled=True)  89.4 us
    all_gather x1, waiting for transfers between devices, per_device(): piece = lax.all_gather(qkv_weight[0], 'lon', axis=0, tiled=True)  40.4 us
    all_gather x1, waiting for transfers between devices, per_device(): lax.all_gather(out_weight[0], 'lon', axis=1, tiled=True)  23.2 us
    ppermute x2, waiting for transfers between devices, from_behind(): return lax.ppermute(block, axis, route)  19.2 us
    dot_general x1, matrix products, per_device(): jnp.dot(hidden, lax.all_gather(down_weight[0], 'lon', axis=1, tiled=True)...  10.1 us
  transfers between devices with their start and end apart: 9, of which 9 were waited for; matrix products, arithmetic and copies ran while one was open for 5% of the time, Pallas kernels for 0%

commit v1 on v0

--- a/solution.py
+++ b/solution.py
@@ -1,6 +1,10 @@
+import functools
+
 import jax
 import jax.numpy as jnp
 from jax import lax
+from jax.experimental import pallas as pl
+from jax.experimental.pallas import tpu as pltpu
 from jax.sharding import PartitionSpec as P
 
 W = 8
@@ -61,6 +65,158 @@
     weights = (raw_weights / jnp.sum(raw_weights, axis=-1, keepdims=True)).astype(jnp.bfloat16)
     context = jnp.einsum("whij,wjhd->wihd", weights, value_rows, preferred_element_type=jnp.float32)
     return context.astype(jnp.bfloat16)
+
+
+MESH = pl.DeviceIdType.MESH
+TILE_ROWS = 16
+SPLITS = (2, 2, 2, 1)
+AHEAD = 2
+
+
+def relay_kernel(count, *refs):
+    kinds = len(SPLITS)
+    shards, wholes = refs[:kinds], refs[kinds : 2 * kinds]
+    hop_send, hop_recv, side_send, side_recv, own_sem = refs[2 * kinds :]
+    place = lax.axis_index("lon")
+    half = lax.axis_index("grp")
+    pieces = [(kind, part) for kind in range(kinds) for part in range(SPLITS[kind])]
+
+    def rows_of(piece, side):
+        kind, part = pieces[piece]
+        length = shards[kind].shape[0] // (2 * SPLITS[kind])
+        start = pl.multiple_of((side * SPLITS[kind] + part) * length, TILE_ROWS)
+        return kind, pl.ds(start, length)
+
+    def hop(piece, way, origin, own):
+        kind, rows = rows_of(piece, half)
+        target = wholes[kind].at[origin, rows]
+        index = 0 if way > 0 else 1
+        return pltpu.make_async_remote_copy(
+            src_ref=shards[kind].at[rows] if own else target,
+            dst_ref=target,
+            send_sem=hop_send.at[index, piece, origin],
+            recv_sem=hop_recv.at[index, piece, origin],
+            device_id={"lon": jnp.clip(place + way, 0, count - 1)},
+            device_id_type=MESH,
+        )
+
+    def across(piece, origin, side):
+        kind, rows = rows_of(piece, side)
+        target = wholes[kind].at[origin, rows]
+        return pltpu.make_async_remote_copy(
+            src_ref=target,
+            dst_ref=target,
+            send_sem=side_send.at[piece, origin],
+            recv_sem=side_recv.at[piece, origin],
+            device_id={"grp": 1 - half},
+            device_id_type=MESH,
+        )
+
+    def has(way):
+        return place < count - 1 if way > 0 else place > 0
+
+    barrier = pltpu.get_barrier_semaphore()
+    for way in (1, -1):
+
+        @pl.when(has(way))
+        def _():
+            pl.semaphore_signal(
+                barrier, inc=1, device_id={"lon": place + way}, device_id_type=MESH
+            )
+
+    pl.semaphore_signal(barrier, inc=1, device_id={"grp": 1 - half}, device_id_type=MESH)
+    pl.semaphore_wait(barrier, 1 + jnp.where(has(1), 1, 0) + jnp.where(has(-1), 1, 0))
+
+    def send_own(piece):
+        for way in (1, -1):
+
+            @pl.when(has(way))
+            def _():
+                hop(piece, way, place, True).start()
+
+    for piece in range(AHEAD):
+        send_own(piece)
+    own = [
+        pltpu.make_async_copy(shards[kind], wholes[kind].at[place], own_sem.at[kind])
+        for kind in range(kinds)
+    ]
+    for copy in own:
+        copy.start()
+    for piece in range(len(pieces)):
+        if piece + AHEAD < len(pieces):
+            send_own(piece + AHEAD)
+
+        def step(distance, carry):
+            for way in (1, -1):
+                origin = place - distance * way
+
+                @pl.when((origin >= 0) & (origin < count))
+                def _():
+                    hop(piece, way, origin, False).wait_recv()
+
+                    @pl.when(has(way))
+                    def _():
+                        hop(piece, way, origin, False).start()
+
+                    across(piece, origin, half).start()
+
+            return carry
+
+        lax.fori_loop(1, count, step, 0)
+    for copy in own:
+        copy.wait()
+    for piece in range(len(pieces)):
+
+        def drain(origin, carry):
+            @pl.when(origin != place)
+            def _():
+                across(piece, origin, 1 - half).wait_recv()
+                across(piece, origin, half).wait_send()
+
+            for way in (1, -1):
+
+                @pl.when(has(way) & ((place - origin) * way >= 0))
+                def _():
+                    hop(piece, way, origin, False).wait_send()
+
+            return carry
+
+        lax.fori_loop(0, count, drain, 0)
+
+
+def relayed(shards):
+    count = lax.axis_size("lon")
+    pieces = sum(SPLITS)
+    return pl.pallas_call(
+        functools.partial(relay_kernel, count),
+        out_shape=[jax.ShapeDtypeStruct((count,) + w.shape, w.dtype) for w in shards],
+        in_specs=[pl.BlockSpec(memory_space=pl.ANY)] * len(shards),
+        out_specs=[pl.BlockSpec(memory_space=pl.ANY)] * len(shards),
+        scratch_shapes=[
+            pltpu.SemaphoreType.DMA((2, pieces, count)),
+            pltpu.SemaphoreType.DMA((2, pieces, count)),
+            pltpu.SemaphoreType.DMA((pieces, count)),
+            pltpu.SemaphoreType.DMA((pieces, count)),
+            pltpu.SemaphoreType.DMA((len(shards),)),
+        ],
+        compiler_params=pltpu.CompilerParams(collective_id=0, has_side_effects=True),
+    )(*shards)
+
+
+def gathered_weights(shards):
+    fits = all(w.shape[0] % (2 * n * TILE_ROWS) == 0 for w, n in zip(shards, SPLITS))
+    if fits and lax.axis_size("grp") == 2:
+        return relayed(shards)
+    return [lax.all_gather(w, "lon", axis=0, tiled=False) for w in shards]
+
+
+def by_rows(whole):
+    return whole.reshape(-1, whole.shape[2])
+
+
+def times_columns(left, whole):
+    terms = jnp.einsum("th,lhc->tlc", left, whole, preferred_element_type=jnp.float32)
+    return terms.reshape(left.shape[0], -1)
 
 
 def per_device(
@@ -78,23 +234,22 @@
     out_weight,
     attn_gain,
 ):
+    qkv_flat = qkv_weight[0].reshape(qkv_weight.shape[1], -1)
+    up_whole, down_whole, qkv_whole, out_whole = gathered_weights(
+        [up_weight[0], down_weight[0], qkv_flat, out_weight[0]]
+    )
     tile_in = section_input[0]
     height, breadth, width = tile_in.shape
     gathered = lax.all_gather(tile_in, "lat", axis=0, tiled=True)
     flat_rows = gathered.reshape(-1, width)
-    up_local = up_weight[0]
     columns = flat_rows
     pre_act = jnp.dot(
         columns,
-        lax.all_gather(up_local, "lon", axis=0, tiled=True),
+        by_rows(up_whole),
         preferred_element_type=jnp.float32,
     )
     hidden = jax.nn.gelu(pre_act + up_bias[0], approximate=False).astype(jnp.bfloat16)
-    down_terms = jnp.dot(
-        hidden,
-        lax.all_gather(down_weight[0], "lon", axis=1, tiled=True),
-        preferred_element_type=jnp.float32,
-    )
+    down_terms = times_columns(hidden, down_whole)
     mlp_sum = lax.psum_scatter(
         down_terms.astype(jnp.bfloat16), "lat", scatter_dimension=0, tiled=True
     ).astype(jnp.float32)
@@ -120,19 +275,14 @@
     flat_grid = grid.reshape(-1, width)
     heads_local = logit_scale.shape[1]
     head_size = qkv_weight.shape[3] // heads_local
-    piece = lax.all_gather(qkv_weight[0], "lon", axis=0, tiled=True)
     columns = flat_grid
-    packed = jnp.dot(columns, piece.reshape(piece.shape[0], -1), preferred_element_type=jnp.float32)
+    packed = jnp.dot(columns, by_rows(qkv_whole), preferred_element_type=jnp.float32)
     packed = packed.astype(jnp.bfloat16).reshape(grid_height, breadth, 3, heads_local, head_size)
     context = attend(packed, grid_marks, logit_scale[0], position_bias[0])
     context = unwindow(context, grid_height, breadth, W).reshape(
         grid_height * breadth, heads_local * head_size
     )
-    out_terms = jnp.dot(
-        context,
-        lax.all_gather(out_weight[0], "lon", axis=1, tiled=True),
-        preferred_element_type=jnp.float32,
-    )
+    out_terms = times_columns(context, out_whole)
     out_terms = jnp.roll(out_terms.reshape(grid_height, breadth, width), shift_lat, axis=0).reshape(
         -1, width
     )

time: 348 us -> 254 us (0.73)
  waiting for transfers between devices: 276 us -> 26.1 us
  Pallas kernels: 0 us -> 144 us
  local copies, waits for them, and re-layouts: 6.41 us -> 15.4 us
    all_gather x4 -> x0, waiting for transfers between devices: 244 us -> none  [the longest x1 90.5 us: per_device(): lax.all_gather(up_local, 'lon', axis=0, tiled=True)]
    pallas_call x0 -> x1, Pallas kernels: none -> 144 us  [relayed(): pl.pallas_call(functools.partial(relay_kernel, count), out_shape=[jax.Sha...]
    ppermute x2, waiting for transfers between devices: 19.2 us -> 9.98 us  [from_behind(): return lax.ppermute(block, axis, route)]
  transfers between devices with their start and end apart: 9 -> 5, of which waited for: 9 -> 4; matrix products, arithmetic and copies ran while one was open for 5% -> 2% of each run, Pallas kernels for 0% -> 0%
where the time goes in v1:
time: 254 us; the launch traced here: 253 us
  Pallas kernels  144 us (57%)
  waiting for transfers between devices  26.1 us (10%)
  between operations  20.2 us (8%)
  matrix products  17.6 us (7%)
  local copies, waits for them, and re-layouts  15.4 us (6%)
  other arithmetic  13.8 us (5%)
  starting transfers between devices  9.73 us (4%)
  blocking collectives  6.75 us (3%)
    pallas_call x1, Pallas kernels, relayed(): pl.pallas_call(functools.partial(relay_kernel, count), out_shape=[jax.Sha...  144 us
    dot_general x2, matrix products, times_columns(): jnp.einsum('th,lhc->tlc', left, whole, preferred_element_type=jnp.float32)  12.4 us
    ppermute x2, waiting for transfers between devices, from_behind(): return lax.ppermute(block, axis, route)  9.98 us
    reduce_scatter x1, waiting for transfers between devices, per_device(): lax.psum_scatter(out_terms.astype(jnp.bfloat16), 'lat', scatter_dimension...  9.75 us
    reduce_scatter x1, waiting for transfers between devices, per_device(): lax.psum_scatter(down_terms.astype(jnp.bfloat16), 'lat', scatter_dimensio...  6.35 us
    ppermute x2, starting transfers between devices, from_behind(): return lax.ppermute(block, axis, route)  5.18 us
  transfers between devices with their start and end apart: 5, of which 4 were waited for; matrix products, arithmetic and copies ran while one was open for 2% of the time, Pallas kernels for 0%

profile of v1, /device:TPU:0, one launch (start us, length us, event | category | flops | bytes accessed | tf_op | source)
XLA Modules:
  0.0 253.2 jit_solution(9166165452470261400)
XLA Ops:
  7.2 2.5 copy.52
  9.8 1.5 copy.53.refs_2_
  11.3 2.4 all-gather
  13.8 143.6 %shard_map.140 = (bf16[4,384,1536]{2,1,0:T(8,128)(2,1)}, bf16[4,1536,384]{2,1,0:T(8,128)(2,1)}, bf16[4,384,1152]{2,1,0:T(8,128)(2,1)}, bf16[4,384,384]{2,1,0:T(8,128)(2,1)}) custom-call(bf16[384,1536]{1,0:T(8,128)(2,1)} %bitcast.147, bf16[1536,384]{1,0:T(8,128)(2,1)} %bitcast.148, bf16[384,1152]{1,0:T(8,128)(2,1)} %copy.53.refs_2_, bf16[384,384]{1,0:T(8,128)(2,1)} %bitcast.150), custom_call_target="tpu_custom_call" | custom-call | tf_op jit(solution)/shard_map/pallas_call | solution.py:190
  157.3 11.8 %convolution_convert_fusion.1 = bf16[256,4,384]{2,0,1:T(8,128)(2,1)S(1)} fusion(bf16[4,1536,384]{2,1,0:T(8,128)(2,1)} %get-tuple-element.7, bf16[1536,1536]{1,0:T(8,128)(2,1)} %bitcast.152, bf16[1,32,8,1536]{3,2,0,1:T(8,128)(2,1)S(1)} %all-gather, f32[1536]{0:T(1024)S(1)} %reduce), kind=kOutput, calls=%fused_computation.33 | convolution fusion | flops 2442264576 | bytes 11016192 | tf_op jit(solution)/shard_map/th,lhc->tlc/dot_general | solution.py:218
  170.7 6.3 %reduce-scatter.3.cloned.1.call-done = bf16[128,1536]{1,0:T(8,128)(2,1)} async-done(((bf16[256,1536]{1,0:T(8,128)(2,1)}), bf16[128,1536]{1,0:T(8,128)(2,1)}) %reduce-scatter.3.cloned.1.call-update) | async-done | bytes 393232 | tf_op jit(solution)/shard_map/reduce_scatter | solution.py:253
  178.2 1.2 fusion.34
  180.0 1.3 fusion.106
  181.3 4.5 %collective-permute-start = (bf16[16,8,1536]{2,1,0:T(8,128)(2,1)S(1)}, bf16[16,8,1536]{2,1,0:T(8,128)(2,1)}, u32[]{:S(2)}, u32[]{:S(2)}) collective-permute-start(bf16[16,8,1536]{2,1,0:T(8,128)(2,1)S(1)} %fusion.106), channel_id=1, source_target_pairs={{0,8},{1,9},{2,10},{3,11},{4,12},{5,13},{6,14},{7,15},{16,24},{17,... | collective-permute-start | bytes 1179656 | tf_op jit(solution)/shard_map/ppermute | solution.py:16
  191.1 1.8 all-gather.1
  194.7 3.4 %collective-permute-start.1 = (bf16[16,4,1536]{2,1,0:T(4,128)(2,1)S(1)}, bf16[16,4,1536]{2,1,0:T(4,128)(2,1)S(1)}, u32[]{:S(2)}, u32[]{:S(2)}) collective-permute-start(bf16[16,4,1536]{2,1,0:T(4,128)(2,1)S(1)} %slice.28), channel_id=1, source_target_pairs={{1,0},{2,1},{3,2},{0,3},{5,4},{6,5},{7,6},{4,7},{9,8},{10,9},{11,1... | collective-permute-start | bytes 589832 | tf_op jit(solution)/shard_map/ppermute | solution.py:22
  198.8 3.8 %collective-permute-done.1 = bf16[16,4,1536]{2,1,0:T(4,128)(2,1)S(1)} collective-permute-done((bf16[16,4,1536]{2,1,0:T(4,128)(2,1)S(1)}, bf16[16,4,1536]{2,1,0:T(4,128)(2,1)S(1)}, u32[]{:S(2)}, u32[]{:S(2)}) %collective-permute-start.1) | collective-permute-done | bytes 196640 | tf_op jit(solution)/shard_map/ppermute | solution.py:22
  202.9 2.5 %all_gather.10 = bf16[32,8,1536]{2,1,0:T(8,128)(2,1)S(1)} all-gather(bf16[16,8,1536]{2,1,0:T(8,128)(2,1)S(1)} %fusion.58), channel_id=1, replica_groups=mesh['grp'=2,'section'=2,'lat'=2,'lon'=4] {'lat'}, dimensions={0}, use_global_device_ids=true | all-gather | bytes 1179648 | tf_op jit(solution)/shard_map/all_gather | solution.py:270
  205.5 1.4 convolution_convert_fusion
  207.9 2.2 reshape_transpose_reshape_reshape.3
  210.1 1.4 fusion.97
  211.5 1.3 copy.72
  215.0 2.2 fusion.25
  217.2 1.6 fusion.26
  222.7 9.7 %reduce-scatter.5.cloned.1.call-done = bf16[128,1536]{1,0:T(8,128)(2,1)} async-done(((bf16[256,1536]{1,0:T(8,128)(2,1)}), bf16[128,1536]{1,0:T(8,128)(2,1)}) %reduce-scatter.5.cloned.1.call-update) | async-done | bytes 393232 | tf_op jit(solution)/shard_map/reduce_scatter | solution.py:289
  233.6 1.2 fusion.31
  234.8 1.3 fusion.59
  236.2 1.8 collective-permute-start.2
  239.1 6.2 %collective-permute-done.2 = bf16[16,4,1536]{2,1,0:T(4,128)(2,1)S(1)} collective-permute-done((bf16[16,4,1536]{2,1,0:T(4,128)(2,1)S(1)}, bf16[16,4,1536]{2,1,0:T(4,128)(2,1)S(1)}, u32[]{:S(2)}, u32[]{:S(2)}) %collective-permute-start.2) | collective-permute-done | bytes 196640 | tf_op jit(solution)/shard_map/ppermute | solution.py:22
  (68 shorter events, 16.0 us)
Async XLA Ops:
  7.2 4.1 %copy-start.1 = (bf16[1,16,8,1536]{3,2,1,0:T(8,128)(2,1)S(1)}, bf16[1,16,8,1536]{3,2,1,0:T(8,128)(2,1)}, u32[]{:S(2)}) copy-start(bf16[1,16,8,1536]{3,2,1,0:T(8,128)(2,1)} %param.13) | copy-start | bytes 1179652
  7.2 169.9 %reduce-scatter.3.cloned.1.call-start = ((), (), s32[]{:S(2)}) async-start(), calls=%async_computation.2 | async-start | bytes 1179648 | tf_op jit(solution)/shard_map/reduce_scatter | solution.py:253
  9.8 4.0 %copy-start.6 = (f32[1,1536]{1,0:T(1,128)S(1)}, f32[1,1536]{1,0:T(1,128)}, u32[]{:S(2)}) copy-start(f32[1,1536]{1,0:T(1,128)} %param.18) | copy-start | bytes 18436
  169.4 1.3 copy-start.7
  170.6 15.2 %copy-start.12 = (s32[2]{0:T(128)S(1)}, s32[2]{0:T(128)}, u32[]{:S(2)}) copy-start(s32[2]{0:T(128)} %param.15) | copy-start | bytes 28
  170.6 19.8 %copy-start.5 = (f32[1,6,64,64]{3,2,1,0:T(8,128)S(1)}, f32[1,6,64,64]{3,2,1,0:T(8,128)}, u32[]{:S(2)}) copy-start(f32[1,6,64,64]{3,2,1,0:T(8,128)} %param.23) | copy-start | bytes 294916
  170.6 20.6 %copy-start.9 = (s32[16,8]{0,1:T(8,128)S(1)}, s32[16,8]{0,1:T(8,128)}, u32[]{:S(2)}) copy-start(s32[16,8]{0,1:T(8,128)} %param.16) | copy-start | bytes 1540
  170.6 22.5 %copy-start.2 = (bf16[4,384,384]{2,1,0:T(8,128)(2,1)S(1)}, bf16[4,384,384]{2,1,0:T(8,128)(2,1)}, u32[]{:S(2)}) copy-start(bf16[4,384,384]{2,1,0:T(8,128)(2,1)} %get-tuple-element.9) | copy-start | bytes 3538948
  170.6 61.8 %reduce-scatter.5.cloned.1.call-start = ((), (), s32[]{:S(2)}) async-start(), calls=%async_computation.3 | async-start | bytes 1179648 | tf_op jit(solution)/shard_map/reduce_scatter | solution.py:289
  179.4 0.5 copy-start.10
  181.3 13.2 %copy-start.4 = (bf16[16,8,1536]{2,1,0:T(8,128)(2,1)S(1)}, bf16[16,8,1536]{2,1,0:T(8,128)(2,1)}, u32[]{:S(2)}) copy-start(bf16[16,8,1536]{2,1,0:T(8,128)(2,1)} %param.14) | copy-start | bytes 1179652
  181.3 13.2 %collective-permute-start = (bf16[16,8,1536]{2,1,0:T(8,128)(2,1)S(1)}, bf16[16,8,1536]{2,1,0:T(8,128)(2,1)}, u32[]{:S(2)}, u32[]{:S(2)}) collective-permute-start(bf16[16,8,1536]{2,1,0:T(8,128)(2,1)S(1)} %fusion.106), channel_id=1, source_target_pairs={{0,8},{1,9},{2,10},{3,11},{4,12},{5,13},{6,14},{7,15},{16,24},{17,... | collective-permute-start | bytes 1179656 | tf_op jit(solution)/shard_map/ppermute | solution.py:16
  194.5 11.0 %copy-start.13 = (bf16[4,384,1152]{2,1,0:T(8,128)(2,1)S(1)}, bf16[4,384,1152]{2,1,0:T(8,128)(2,1)}, u32[]{:S(2)}) copy-start(bf16[4,384,1152]{2,1,0:T(8,128)(2,1)} %get-tuple-element.8) | copy-start | bytes 10616836
  194.7 7.9 %collective-permute-start.1 = (bf16[16,4,1536]{2,1,0:T(4,128)(2,1)S(1)}, bf16[16,4,1536]{2,1,0:T(4,128)(2,1)S(1)}, u32[]{:S(2)}, u32[]{:S(2)}) collective-permute-start(bf16[16,4,1536]{2,1,0:T(4,128)(2,1)S(1)} %slice.28), channel_id=1, source_target_pairs={{1,0},{2,1},{3,2},{0,3},{5,4},{6,5},{7,6},{4,7},{9,8},{10,9},{11,1... | collective-permute-start | bytes 589832 | tf_op jit(solution)/shard_map/ppermute | solution.py:22
  211.5 3.5 %copy-start.14 = (f32[1,6]{1,0:T(1,128)S(1)}, f32[1,6]{1,0:T(1,128)}, u32[]{:S(2)}) copy-start(f32[1,6]{1,0:T(1,128)} %param.22) | copy-start | bytes 76
  213.7 3.5 %copy-start.3 = (bf16[4,64,1,6,64]{1,0,4,3,2:T(4,128)(2,1)S(1)}, bf16[4,64,1,6,64]{1,0,4,3,2:T(4,128)(2,1)}, u32[]{:S(2)}) copy-start(bf16[4,64,1,6,64]{1,0,4,3,2:T(4,128)(2,1)} %get-tuple-element.12) | copy-start | bytes 589828
  220.1 1.2 copy-start.8
  221.3 16.7 %copy-start = (bf16[128,1536]{1,0:T(8,128)(2,1)S(1)}, bf16[128,1536]{1,0:T(8,128)(2,1)}, u32[]{:S(2)}) copy-start(bf16[128,1536]{1,0:T(8,128)(2,1)} %reduce-scatter.3.cloned.1.call-done) | copy-start | bytes 1179652
  221.3 16.7 %copy-start.11 = (f32[128]{0:T(128)S(1)}, f32[128]{0:T(128)}, u32[]{:S(2)}) copy-start(f32[128]{0:T(128)} %copy-done.10) | copy-start | bytes 1540
  236.2 9.0 %collective-permute-start.2 = (bf16[16,4,1536]{2,1,0:T(4,128)(2,1)S(1)}, bf16[16,4,1536]{2,1,0:T(4,128)(2,1)S(1)}, u32[]{:S(2)}, u32[]{:S(2)}) collective-permute-start(bf16[16,4,1536]{2,1,0:T(4,128)(2,1)S(1)} %slice.32), channel_id=1, source_target_pairs={{3,0},{0,1},{1,2},{2,3},{7,4},{4,5},{5,6},{6,7},{11,8},{8,9},{9,10... | collective-permute-start | bytes 589832 | tf_op jit(solution)/shard_map/ppermute | solution.py:22
Sparse Core Ops, SparseCore 0:
  170.7 6.2 reduce-scatter.2
  221.4 10.9 reduce-scatter.4

commit v2 on v1

--- a/solution.py
+++ b/solution.py
@@ -45,10 +45,7 @@
 
 
 def attend(packed, region_marks, head_scale, pos_bias):
-    blocks = windows(packed, W)
-    query_rows = blocks[:, :, 0]
-    key_rows = blocks[:, :, 1]
-    value_rows = blocks[:, :, 2]
+    query_rows, key_rows, value_rows = [windows(packed[kind], W) for kind in range(3)]
     inner_dot = jnp.einsum(
         "wihd,wjhd->whij", query_rows, key_rows, preferred_element_type=jnp.float32
     )
@@ -70,29 +67,58 @@
 MESH = pl.DeviceIdType.MESH
 TILE_ROWS = 16
 SPLITS = (2, 2, 2, 1)
-AHEAD = 2
-
-
-def relay_kernel(count, *refs):
+AHEAD = 3
+UP_READY = 3
+DOWN_READY = 5
+VMEM_BYTES = 40 * 2**20
+
+
+def relay_kernel(count, sections, *refs):
     kinds = len(SPLITS)
-    shards, wholes = refs[:kinds], refs[kinds : 2 * kinds]
-    hop_send, hop_recv, side_send, side_recv, own_sem = refs[2 * kinds :]
+    shards = refs[:kinds]
+    tokens, bias, tile, gain, fresh, handed, entering, qkv_whole, out_whole = refs[
+        kinds : kinds + 9
+    ]
+    (
+        up_whole,
+        down_whole,
+        hidden,
+        own_terms,
+        sent_terms,
+        peer_terms,
+        hop_send,
+        hop_recv,
+        side_send,
+        side_recv,
+        own_sem,
+        term_send,
+        term_recv,
+        hand_sem,
+    ) = refs[kinds + 9 :]
+    wholes = (up_whole, down_whole, qkv_whole, out_whole)
     place = lax.axis_index("lon")
     half = lax.axis_index("grp")
+    row_half = lax.axis_index("lat")
+    section = lax.axis_index("section")
     pieces = [(kind, part) for kind in range(kinds) for part in range(SPLITS[kind])]
 
     def rows_of(piece, side):
         kind, part = pieces[piece]
-        length = shards[kind].shape[0] // (2 * SPLITS[kind])
-        start = pl.multiple_of((side * SPLITS[kind] + part) * length, TILE_ROWS)
-        return kind, pl.ds(start, length)
+        length = shards[kind].shape[1] // (2 * SPLITS[kind])
+        return kind, (side * SPLITS[kind] + part) * length, length
+
+    def target_of(piece, origin, side):
+        kind, start, length = rows_of(piece, side)
+        first = pl.multiple_of(origin * shards[kind].shape[1] + start, TILE_ROWS)
+        return wholes[kind].at[:, pl.ds(first, length)]
 
     def hop(piece, way, origin, own):
-        kind, rows = rows_of(piece, half)
-        target = wholes[kind].at[origin, rows]
+        kind, start, length = rows_of(piece, half)
+        target = target_of(piece, origin, half)
+        source = shards[kind].at[:, pl.ds(pl.multiple_of(start, TILE_ROWS), length)]
         index = 0 if way > 0 else 1
         return pltpu.make_async_remote_copy(
-            src_ref=shards[kind].at[rows] if own else target,
+            src_ref=source if own else target,
             dst_ref=target,
             send_sem=hop_send.at[index, piece, origin],
             recv_sem=hop_recv.at[index, piece, origin],
@@ -101,8 +127,7 @@
         )
 
     def across(piece, origin, side):
-        kind, rows = rows_of(piece, side)
-        target = wholes[kind].at[origin, rows]
+        target = target_of(piece, origin, side)
         return pltpu.make_async_remote_copy(
             src_ref=target,
             dst_ref=target,
@@ -115,6 +140,9 @@
     def has(way):
         return place < count - 1 if way > 0 else place > 0
 
+    def has_section(way):
+        return section < sections - 1 if way > 0 else section > 0
+
     barrier = pltpu.get_barrier_semaphore()
     for way in (1, -1):
 
@@ -124,8 +152,18 @@
                 barrier, inc=1, device_id={"lon": place + way}, device_id_type=MESH
             )
 
+        @pl.when(has_section(way))
+        def _():
+            pl.semaphore_signal(
+                barrier, inc=1, device_id={"section": section + way}, device_id_type=MESH
+            )
+
     pl.semaphore_signal(barrier, inc=1, device_id={"grp": 1 - half}, device_id_type=MESH)
-    pl.semaphore_wait(barrier, 1 + jnp.where(has(1), 1, 0) + jnp.where(has(-1), 1, 0))
+    pl.semaphore_signal(barrier, inc=1, device_id={"lat": 1 - row_half}, device_id_type=MESH)
+    greeted = 2
+    for way in (1, -1):
+        greeted = greeted + jnp.where(has(way), 1, 0) + jnp.where(has_section(way), 1, 0)
+    pl.semaphore_wait(barrier, greeted)
 
     def send_own(piece):
         for way in (1, -1):
@@ -134,17 +172,120 @@
             def _():
                 hop(piece, way, place, True).start()
 
+    def term_copy():
+        return pltpu.make_async_remote_copy(
+            src_ref=sent_terms,
+            dst_ref=peer_terms,
+            send_sem=term_send,
+            recv_sem=term_recv,
+            device_id={"lat": 1 - row_half},
+            device_id_type=MESH,
+        )
+
+    def hand_copy():
+        return pltpu.make_async_remote_copy(
+            src_ref=handed,
+            dst_ref=entering,
+            send_sem=hand_sem.at[0],
+            recv_sem=hand_sem.at[1],
+            device_id={"section": jnp.clip(section + 1, 0, sections - 1)},
+            device_id_type=MESH,
+        )
+
+    def fresh_copy():
+        return pltpu.make_async_copy(fresh, entering, hand_sem.at[2])
+
+    def await_across(kind):
+        own[kind].wait()
+        for piece in range(len(pieces)):
+            if pieces[piece][0] == kind:
+
+                def arrive(origin, carry):
+                    @pl.when(origin != place)
+                    def _():
+                        across(piece, origin, 1 - half).wait_recv()
+
+                    return carry
+
+                lax.fori_loop(0, count, arrive, 0)
+
+    def run_up():
+        width = hidden.shape[1] // 4
+
+        def block(index, carry):
+            columns = pl.ds(pl.multiple_of(index * width, 128), width)
+            total = jnp.dot(
+                tokens[...], up_whole[0, :, columns], preferred_element_type=jnp.float32
+            )
+            total = total + bias[:, columns]
+            total = 0.5 * total * (1.0 + lax.erf(total * (0.5**0.5)))
+            hidden[:, columns] = total.astype(hidden.dtype)
+            return carry
+
+        lax.fori_loop(0, 4, block, 0)
+
+    def run_down():
+        height = own_terms.shape[0]
+        depth, width = shards[1].shape[1:]
+
+        def block(whose, result):
+            rows = pl.ds(pl.multiple_of(whose * height, TILE_ROWS), height)
+            for origin in range(count):
+                term = jnp.dot(
+                    hidden[rows, :],
+                    down_whole[0, origin * depth : (origin + 1) * depth, :],
+                    preferred_element_type=jnp.float32,
+                )
+                result[:, origin * width : (origin + 1) * width] = term.astype(result.dtype)
+
+        block(1 - row_half, sent_terms)
+        term_copy().start()
+        block(row_half, own_terms)
+
+    def finish_mlp():
+        term_copy().wait_recv()
+        total = own_terms[...].astype(jnp.float32) + peer_terms[...].astype(jnp.float32)
+        moved = tile[...].astype(jnp.float32) + layer_norm(total, gain[...])
+        handed[...] = moved.astype(handed.dtype)
+
+        @pl.when(has_section(1))
+        def _():
+            hand_copy().start()
+
+    own = [
+        pltpu.make_async_copy(
+            shards[kind],
+            wholes[kind].at[
+                :,
+                pl.ds(
+                    pl.multiple_of(place * shards[kind].shape[1], TILE_ROWS),
+                    shards[kind].shape[1],
+                ),
+            ],
+            own_sem.at[kind],
+        )
+        for kind in range(kinds)
+    ]
     for piece in range(AHEAD):
         send_own(piece)
-    own = [
-        pltpu.make_async_copy(shards[kind], wholes[kind].at[place], own_sem.at[kind])
-        for kind in range(kinds)
-    ]
     for copy in own:
         copy.start()
+
+    @pl.when(jnp.logical_not(has_section(-1)))
+    def _():
+        fresh_copy().start()
+
     for piece in range(len(pieces)):
         if piece + AHEAD < len(pieces):
             send_own(piece + AHEAD)
+        if piece == UP_READY:
+            await_across(0)
+            run_up()
+        if piece == DOWN_READY:
+            await_across(1)
+            run_down()
+        if piece == DOWN_READY + 1:
+            finish_mlp()
 
         def step(distance, carry):
             for way in (1, -1):
@@ -163,14 +304,13 @@
             return carry
 
         lax.fori_loop(1, count, step, 0)
-    for copy in own:
-        copy.wait()
+    await_across(2)
+    await_across(3)
     for piece in range(len(pieces)):
 
         def drain(origin, carry):
             @pl.when(origin != place)
             def _():
-                across(piece, origin, 1 - half).wait_recv()
                 across(piece, origin, half).wait_send()
 
             for way in (1, -1):
@@ -182,39 +322,80 @@
             return carry
 
         lax.fori_loop(0, count, drain, 0)
-
-
-def relayed(shards):
+    term_copy().wait_send()
+
+    @pl.when(has_section(1))
+    def _():
+        hand_copy().wait_send()
+
+    @pl.when(has_section(-1))
+    def _():
+        hand_copy().wait_recv()
+
+    @pl.when(jnp.logical_not(has_section(-1)))
+    def _():
+        fresh_copy().wait()
+
+
+def relayed(shards, tokens, bias, tile, gain, fresh):
     count = lax.axis_size("lon")
     pieces = sum(SPLITS)
+    wholes = [
+        jax.ShapeDtypeStruct((w.shape[0], count * w.shape[1], w.shape[2]), w.dtype)
+        for w in shards
+    ]
+    near = pl.BlockSpec(memory_space=pltpu.VMEM)
+    far = pl.BlockSpec(memory_space=pl.ANY)
     return pl.pallas_call(
-        functools.partial(relay_kernel, count),
-        out_shape=[jax.ShapeDtypeStruct((count,) + w.shape, w.dtype) for w in shards],
-        in_specs=[pl.BlockSpec(memory_space=pl.ANY)] * len(shards),
-        out_specs=[pl.BlockSpec(memory_space=pl.ANY)] * len(shards),
+        functools.partial(relay_kernel, count, lax.axis_size("section")),
+        out_shape=[jax.ShapeDtypeStruct(tile.shape, tile.dtype)] * 2 + wholes[2:],
+        in_specs=[far] * len(shards) + [near] * 4 + [far],
+        out_specs=[near, far, far, far],
         scratch_shapes=[
+            pltpu.VMEM(wholes[0].shape, wholes[0].dtype),
+            pltpu.VMEM(wholes[1].shape, wholes[1].dtype),
+            pltpu.VMEM((tokens.shape[0], shards[0].shape[2]), tile.dtype),
+            pltpu.VMEM(tile.shape, tile.dtype),
+            pltpu.VMEM(tile.shape, tile.dtype),
+            pltpu.VMEM(tile.shape, tile.dtype),
             pltpu.SemaphoreType.DMA((2, pieces, count)),
             pltpu.SemaphoreType.DMA((2, pieces, count)),
             pltpu.SemaphoreType.DMA((pieces, count)),
             pltpu.SemaphoreType.DMA((pieces, count)),
             pltpu.SemaphoreType.DMA((len(shards),)),
+            pltpu.SemaphoreType.DMA,
+            pltpu.SemaphoreType.DMA,
+            pltpu.SemaphoreType.DMA((3,)),
         ],
-        compiler_params=pltpu.CompilerParams(collective_id=0, has_side_effects=True),
-    )(*shards)
-
-
-def gathered_weights(shards):
-    fits = all(w.shape[0] % (2 * n * TILE_ROWS) == 0 for w, n in zip(shards, SPLITS))
-    if fits and lax.axis_size("grp") == 2:
-        return relayed(shards)
-    return [lax.all_gather(w, "lon", axis=0, tiled=False) for w in shards]
-
-
-def by_rows(whole):
-    return whole.reshape(-1, whole.shape[2])
+        compiler_params=pltpu.CompilerParams(
+            collective_id=0, has_side_effects=True, vmem_limit_bytes=VMEM_BYTES
+        ),
+    )(*shards, tokens, bias, tile, gain, fresh)
+
+
+def gathered(shards, tokens, bias, tile, gain, fresh):
+    up_whole, down_whole, qkv_whole, out_whole = [
+        lax.all_gather(w, "lon", axis=1, tiled=True) for w in shards
+    ]
+    pre_act = jnp.dot(tokens, up_whole[0], preferred_element_type=jnp.float32)
+    hidden = jax.nn.gelu(pre_act + bias, approximate=False).astype(jnp.bfloat16)
+    down_terms = times_columns(hidden, down_whole).astype(jnp.bfloat16)
+    mlp_sum = lax.psum_scatter(down_terms, "lat", scatter_dimension=0, tiled=True)
+    handed = tile.astype(jnp.float32) + layer_norm(mlp_sum.astype(jnp.float32), gain)
+    handed = handed.astype(jnp.bfloat16)
+    passed = shifted(handed, "section", 1)
+    entering = jnp.where(lax.axis_index("section") == 0, fresh, passed)
+    return handed, entering, qkv_whole, out_whole
+
+
+def mlp_and_weights(shards, *rest):
+    fits = all(w.shape[1] % (2 * n * TILE_ROWS) == 0 for w, n in zip(shards, SPLITS))
+    pairs = lax.axis_size("grp") == 2 and lax.axis_size("lat") == 2
+    return relayed(shards, *rest) if fits and pairs else gathered(shards, *rest)
 
 
 def times_columns(left, whole):
+    whole = whole.reshape(lax.axis_size("lon"), -1, whole.shape[2])
     terms = jnp.einsum("th,lhc->tlc", left, whole, preferred_element_type=jnp.float32)
     return terms.reshape(left.shape[0], -1)
 
@@ -234,30 +415,19 @@
     out_weight,
     attn_gain,
 ):
-    qkv_flat = qkv_weight[0].reshape(qkv_weight.shape[1], -1)
-    up_whole, down_whole, qkv_whole, out_whole = gathered_weights(
-        [up_weight[0], down_weight[0], qkv_flat, out_weight[0]]
-    )
     tile_in = section_input[0]
     height, breadth, width = tile_in.shape
-    gathered = lax.all_gather(tile_in, "lat", axis=0, tiled=True)
-    flat_rows = gathered.reshape(-1, width)
-    columns = flat_rows
-    pre_act = jnp.dot(
-        columns,
-        by_rows(up_whole),
-        preferred_element_type=jnp.float32,
-    )
-    hidden = jax.nn.gelu(pre_act + up_bias[0], approximate=False).astype(jnp.bfloat16)
-    down_terms = times_columns(hidden, down_whole)
-    mlp_sum = lax.psum_scatter(
-        down_terms.astype(jnp.bfloat16), "lat", scatter_dimension=0, tiled=True
-    ).astype(jnp.float32)
-    handed_flat = tile_in.reshape(-1, width).astype(jnp.float32) + layer_norm(mlp_sum, mlp_gain[0])
-    handed = handed_flat.astype(jnp.bfloat16).reshape(height, breadth, width)
-    passed = shifted(handed, "section", 1)
-    first_section = lax.axis_index("section") == 0
-    entering = jnp.where(first_section, fresh_input, passed)
+    token_rows = lax.all_gather(tile_in, "lat", axis=0, tiled=True).reshape(-1, width)
+    handed, entering, qkv_whole, out_whole = mlp_and_weights(
+        [up_weight, down_weight, jnp.swapaxes(qkv_weight[0], 0, 1), out_weight],
+        token_rows,
+        up_bias,
+        tile_in.reshape(-1, width),
+        mlp_gain,
+        fresh_input.reshape(-1, width),
+    )
+    handed = handed.reshape(height, breadth, width)
+    entering = entering.reshape(height, breadth, width)
     shift_lat = offsets[0]
     shift_lon = offsets[1]
     strip_width = W // 2
@@ -275,9 +445,8 @@
     flat_grid = grid.reshape(-1, width)
     heads_local = logit_scale.shape[1]
     head_size = qkv_weight.shape[3] // heads_local
-    columns = flat_grid
-    packed = jnp.dot(columns, by_rows(qkv_whole), preferred_element_type=jnp.float32)
-    packed = packed.astype(jnp.bfloat16).reshape(grid_height, breadth, 3, heads_local, head_size)
+    packed = jnp.einsum("td,kdc->ktc", flat_grid, qkv_whole, preferred_element_type=jnp.float32)
+    packed = packed.astype(jnp.bfloat16).reshape(3, grid_height, breadth, heads_local, head_size)
     context = attend(packed, grid_marks, logit_scale[0], position_bias[0])
     context = unwindow(context, grid_height, breadth, W).reshape(
         grid_height * breadth, heads_local * head_size

time: 254 us -> 221 us (0.87)
  waiting for transfers between devices: 26.1 us -> 11.6 us
  matrix products: 17.6 us -> 7.86 us
  starting transfers between devices: 9.73 us -> 3.23 us
  other arithmetic: 13.8 us -> 7.57 us
  Pallas kernels: 144 us -> 149 us
    dot_general x2 -> x1, matrix products: 12.4 us -> 0.61 us  [times_columns(): jnp.einsum('th,lhc->tlc', left, whole, preferred_element_type=jnp.float32)]
    reduce_scatter x1 -> x0, waiting for transfers between devices: 6.35 us -> none  [per_device(): lax.psum_scatter(down_terms.astype(jnp.bfloat16), 'lat', scatter_dimensio...]
    pallas_call x1, Pallas kernels: 144 us -> 149 us  [relayed(): pl.pallas_call(functools.partial(relay_kernel, count, lax.axis_size('sect...]
    unnamed x33 -> x29, local copies, waits for them, and re-layouts: 4.69 us -> 9.28 us
    ppermute x1 -> x0, starting transfers between devices: 4.47 us -> none  [shifted(): return lax.ppermute(array, axis, pairs)]
    reduce_scatter x1, waiting for transfers between devices: 9.75 us -> 5.67 us  [per_device(): lax.psum_scatter(out_terms.astype(jnp.bfloat16), 'lat', scatter_dimension...]
    ppermute x2, waiting for transfers between devices: 9.98 us -> 5.96 us  [from_behind(): return lax.ppermute(block, axis, route)]
  transfers between devices with their start and end apart: 5 -> 3, of which waited for: 4 -> 2; matrix products, arithmetic and copies ran while one was open for 2% -> 1% of each run, Pallas kernels for 0% -> 0%
where the time goes in v2:
time: 221 us; the launch traced here: 220 us
  Pallas kernels  149 us (67%)
  between operations  20 us (9%)
  local copies, waits for them, and re-layouts  13.8 us (6%)
  waiting for transfers between devices  11.6 us (5%)
  matrix products  7.86 us (4%)
  other arithmetic  7.57 us (3%)
  blocking collectives  6.93 us (3%)
  starting transfers between devices  3.23 us (1%)
    pallas_call x1, Pallas kernels, relayed(): pl.pallas_call(functools.partial(relay_kernel, count, lax.axis_size('sect...  149 us
    unnamed x29, local copies, waits for them, and re-layouts  9.28 us
    ppermute x2, waiting for transfers between devices, from_behind(): return lax.ppermute(block, axis, route)  5.96 us
    reduce_scatter x1, waiting for transfers between devices, per_device(): lax.psum_scatter(out_terms.astype(jnp.bfloat16), 'lat', scatter_dimension...  5.67 us
  transfers between devices with their start and end apart: 3, of which 2 were waited for; matrix products, arithmetic and copies ran while one was open for 1% of the time, Pallas kernels for 0%

profile of v2, /device:TPU:0, one launch (start us, length us, event | category | flops | bytes accessed | tf_op | source)
XLA Modules:
  0.0 219.9 jit_solution(12026491549726260277)
XLA Ops:
  7.2 2.8 %all-gather = bf16[1,32,8,1536]{3,2,0,1:T(8,128)(2,1)S(1)} all-gather(bf16[1,16,8,1536]{3,2,0,1:T(8,128)(2,1)} %bitcast.54), channel_id=2, replica_groups=mesh['grp'=2,'section'=2,'lat'=2,'lon'=4] {'lat'}, dimensions={1}, use_global_device_ids=true | all-gather | bytes 1179648 | tf_op jit(solution)/shard_map/all_gather | solution.py:420
  10.0 1.0 copy-done
  11.0 1.3 copy-done.2
  12.3 1.2 copy-done.3
  13.5 1.0 copy-done.4
  14.4 1.0 copy-done.5
  16.8 148.9 %shard_map.140 = (bf16[128,1536]{1,0:T(8,128)(2,1)S(1)}, bf16[128,1536]{1,0:T(8,128)(2,1)S(1)}, bf16[3,1536,384]{2,1,0:T(8,128)(2,1)S(1)}, bf16[1,1536,384]{2,1,0:T(8,128)(2,1)S(1)}) custom-call(bf16[1,384,1536]{2,1,0:T(8,128)(2,1)S(1)} %copy-done.1, bf16[1,1536,384]{2,1,0:T(8,128)(2,1)S(1)} %copy-done.2, bf16[3,384,384]{2,1,0:T(8,128)(2,1)S(1)} %bitcast.57, ...), custom_call_target="tpu_custom_call" | custom-call | tf_op jit(solution)/shard_map/pallas_call | solution.py:349
  165.7 1.7 copy-done.8
  168.1 1.4 collective-permute-start
  174.0 0.8 copy.38
  174.8 1.8 all-gather.1
  176.8 0.8 copy.42
  179.2 2.4 %all_gather.10 = bf16[32,8,1536]{2,1,0:T(8,128)(2,1)S(1)} all-gather(bf16[16,8,1536]{2,1,0:T(8,128)(2,1)S(1)} %fusion.20), channel_id=1, replica_groups=mesh['grp'=2,'section'=2,'lat'=2,'lon'=4] {'lat'}, dimensions={0}, use_global_device_ids=true | all-gather | bytes 1179648 | tf_op jit(solution)/shard_map/all_gather | solution.py:440
  181.6 3.3 %fusion.7 = bf16[3,256,384]{1,2,0:T(8,128)(2,1)S(1)} fusion(bf16[3,1536,384]{2,1,0:T(8,128)(2,1)} %copy-done.8, s32[]{:T(128)S(6)} %select_n.35, bf16[32,8,1536]{2,1,0:T(8,128)(2,1)S(1)} %all_gather.10), kind=kOutput, calls=%fused_computation.13 | convolution fusion | flops 906657792 | bytes 4915204 | tf_op jit(solution)/shard_map/td,kdc->ktc/dot_general | solution.py:448
  186.3 2.3 %fusion.6 = f32[4,6,64,64]{2,3,1,0:T(8,128)} fusion(bf16[4,64,6,64]{1,0,3,2:T(4,128)(2,1)S(1)} %reshape_transpose_reshape_squeeze.11, bf16[4,64,6,64]{1,0,3,2:T(4,128)(2,1)S(1)} %reshape_transpose_reshape_squeeze.10, f32[6,64,64]{1,2,0:T(8,128)} %copy.38, f32[6]{0:T(128)S(1)} %bitcast.62, f32[4,6,64]{2,1,0:T(8,128)S(1)} %copy.37, ...), kind=kOutput, calls=%fused_computation.12 | convolution fusion | flops 13074432 | bytes 913432 | tf_op jit(solution)/shard_map/wihd,wjhd->whij/dot_general | solution.py:49
  188.5 1.7 fusion.8
  191.5 1.2 fusion.17
  192.7 5.7 %reduce-scatter.2.cloned.1.call-done = bf16[128,1536]{1,0:T(8,128)(2,1)} async-done(((bf16[256,1536]{1,0:T(8,128)(2,1)}), bf16[128,1536]{1,0:T(8,128)(2,1)}) %reduce-scatter.2.cloned.1.call-update) | async-done | bytes 393232 | tf_op jit(solution)/shard_map/reduce_scatter | solution.py:458
  198.4 1.1 convert_reduce_fusion
  199.5 1.2 fusion.11
  200.8 1.3 fusion.21
  202.2 1.8 collective-permute-start.1
  205.2 6.0 %collective-permute-done.1 = bf16[16,4,1536]{2,1,0:T(4,128)(2,1)S(1)} collective-permute-done((bf16[16,4,1536]{2,1,0:T(4,128)(2,1)S(1)}, bf16[16,4,1536]{2,1,0:T(4,128)(2,1)S(1)}, u32[]{:S(2)}, u32[]{:S(2)}) %collective-permute-start.1) | collective-permute-done | bytes 196640 | tf_op jit(solution)/shard_map/ppermute | solution.py:22
  211.2 1.1 fusion.18
  (50 shorter events, 7.4 us)
Async XLA Ops:
  7.2 2.8 %copy-start.1 = (bf16[1,384,1536]{2,1,0:T(8,128)(2,1)S(1)}, bf16[1,384,1536]{2,1,0:T(8,128)(2,1)}, u32[]{:S(2)}) copy-start(bf16[1,384,1536]{2,1,0:T(8,128)(2,1)} %refs_0_.1) | copy-start | bytes 3538948
  7.2 191.2 %reduce-scatter.2.cloned.1.call-start = ((), (), s32[]{:S(2)}) async-start(), calls=%async_computation.1 | async-start | bytes 1179648 | tf_op jit(solution)/shard_map/reduce_scatter | solution.py:458
  10.0 1.0 copy-start
  11.0 1.3 copy-start.2
  12.3 1.2 copy-start.3
  13.4 1.0 copy-start.4
  14.4 1.0 copy-start.5
  15.4 0.7 copy-start.6
  16.1 0.7 copy-start.7
  16.8 152.7 %copy-start.12 = (s32[2]{0:T(128)S(1)}, s32[2]{0:T(128)}, u32[]{:S(2)}) copy-start(s32[2]{0:T(128)} %param.15) | copy-start | bytes 28
  16.8 157.2 %copy-start.9 = (f32[1,6,64,64]{3,2,1,0:T(8,128)S(1)}, f32[1,6,64,64]{3,2,1,0:T(8,128)}, u32[]{:S(2)}) copy-start(f32[1,6,64,64]{3,2,1,0:T(8,128)} %param.23) | copy-start | bytes 294916
  16.8 158.0 %copy-start.11 = (s32[16,8]{0,1:T(8,128)S(1)}, s32[16,8]{0,1:T(8,128)}, u32[]{:S(2)}) copy-start(s32[16,8]{0,1:T(8,128)} %param.16) | copy-start | bytes 1540
  165.7 1.7 copy-start.8
  168.1 10.8 %collective-permute-start = (bf16[16,4,1536]{2,1,0:T(4,128)(2,1)}, bf16[16,4,1536]{2,1,0:T(4,128)(2,1)S(1)}, u32[]{:S(2)}, u32[]{:S(2)}) collective-permute-start(bf16[16,4,1536]{2,1,0:T(4,128)(2,1)} %slice.31), channel_id=1, source_target_pairs={{1,0},{2,1},{3,2},{0,3},{5,4},{6,5},{7,6},{4,7},{9,8},{10,9},{11,1... | collective-permute-start | bytes 589832 | tf_op jit(solution)/shard_map/ppermute | solution.py:22
  185.0 1.2 copy-start.13
  191.4 1.2 copy-start.10
  202.2 9.0 %collective-permute-start.1 = (bf16[16,4,1536]{2,1,0:T(4,128)(2,1)S(1)}, bf16[16,4,1536]{2,1,0:T(4,128)(2,1)S(1)}, u32[]{:S(2)}, u32[]{:S(2)}) collective-permute-start(bf16[16,4,1536]{2,1,0:T(4,128)(2,1)S(1)} %slice.35), channel_id=1, source_target_pairs={{3,0},{0,1},{1,2},{2,3},{7,4},{4,5},{5,6},{6,7},{11,8},{8,9},{9,10... | collective-permute-start | bytes 589832 | tf_op jit(solution)/shard_map/ppermute | solution.py:22
Sparse Core Ops, SparseCore 0:
  192.8 5.5 reduce-scatter.1

commit v3 on v2

--- a/solution.py
+++ b/solution.py
@@ -20,6 +20,25 @@
     devices = range(lax.axis_size(axis))
     route = [((i - distance) % len(devices), i) for i in devices]
     return lax.ppermute(block, axis, route)
+
+
+def turned(grid, first):
+    return lax.dynamic_slice_in_dim(jnp.concatenate([grid, grid], 0), first, grid.shape[0], 0)
+
+
+def summed_over_lat(terms):
+    if lax.axis_size("lat") != 2:
+        total = lax.psum_scatter(terms, "lat", scatter_dimension=0, tiled=True)
+        return total.astype(jnp.float32)
+    me = lax.axis_index("lat")
+    rows = terms.shape[0] // 2
+    kept = lax.dynamic_slice_in_dim(terms, me * rows, rows, 0)
+    given = lax.dynamic_slice_in_dim(terms, (1 - me) * rows, rows, 0)
+    return kept.astype(jnp.float32) + from_behind(given, "lat", 1).astype(jnp.float32)
+
+
+def slab_ids(place, count, shift):
+    return (place >= count - W).astype(jnp.int32) + (place >= count - shift).astype(jnp.int32)
 
 
 def layer_norm(total, norm_gain):
@@ -66,19 +85,18 @@
 
 MESH = pl.DeviceIdType.MESH
 TILE_ROWS = 16
-SPLITS = (2, 2, 2, 1)
+SPLITS = (2, 2, 3, 1)
 AHEAD = 3
 UP_READY = 3
 DOWN_READY = 5
-VMEM_BYTES = 40 * 2**20
+VMEM_BYTES = 60 * 2**20
+BLOCK = 256
 
 
 def relay_kernel(count, sections, *refs):
     kinds = len(SPLITS)
     shards = refs[:kinds]
-    tokens, bias, tile, gain, fresh, handed, entering, qkv_whole, out_whole = refs[
-        kinds : kinds + 9
-    ]
+    bias, tile, gain, fresh, handed, entering, qkv_whole, out_whole = refs[kinds : kinds + 8]
     (
         up_whole,
         down_whole,
@@ -86,6 +104,10 @@
         own_terms,
         sent_terms,
         peer_terms,
+        tokens,
+        mate_tokens,
+        mate_sent,
+        mate_terms,
         hop_send,
         hop_recv,
         side_send,
@@ -94,35 +116,55 @@
         term_send,
         term_recv,
         hand_sem,
-    ) = refs[kinds + 9 :]
+        far_send,
+        mate_sem,
+    ) = refs[kinds + 8 :]
     wholes = (up_whole, down_whole, qkv_whole, out_whole)
     place = lax.axis_index("lon")
     half = lax.axis_index("grp")
     row_half = lax.axis_index("lat")
     section = lax.axis_index("section")
+    parity = lax.rem(place, 2)
+    mate = place + 1 - 2 * parity
+    units = up_whole.shape[2]
     pieces = [(kind, part) for kind in range(kinds) for part in range(SPLITS[kind])]
+
+    def extent(kind):
+        return wholes[kind].shape[1] // count
 
     def rows_of(piece, side):
         kind, part = pieces[piece]
-        length = shards[kind].shape[1] // (2 * SPLITS[kind])
+        length = extent(kind) // (2 * SPLITS[kind])
         return kind, (side * SPLITS[kind] + part) * length, length
+
+    def source_of(kind, start, length, taker):
+        if kind == 0:
+            columns = pl.ds(pl.multiple_of(taker * units, 128), units)
+            return shards[0].at[:, pl.ds(pl.multiple_of(start, TILE_ROWS), length), columns]
+        if kind == 1:
+            start = taker * units + start
+        return shards[kind].at[:, pl.ds(pl.multiple_of(start, TILE_ROWS), length)]
 
     def target_of(piece, origin, side):
         kind, start, length = rows_of(piece, side)
-        first = pl.multiple_of(origin * shards[kind].shape[1] + start, TILE_ROWS)
+        first = pl.multiple_of(origin * extent(kind) + start, TILE_ROWS)
         return wholes[kind].at[:, pl.ds(first, length)]
 
-    def hop(piece, way, origin, own):
+    def hop(piece, way, origin, own, stride):
         kind, start, length = rows_of(piece, half)
         target = target_of(piece, origin, half)
-        source = shards[kind].at[:, pl.ds(pl.multiple_of(start, TILE_ROWS), length)]
         index = 0 if way > 0 else 1
+        if own:
+            source = source_of(kind, start, length, lax.rem(place + stride, 2))
+        else:
+            source = target
+        far_own = own and stride == 2
         return pltpu.make_async_remote_copy(
-            src_ref=source if own else target,
+            src_ref=source,
             dst_ref=target,
-            send_sem=hop_send.at[index, piece, origin],
+            send_sem=far_send.at[index, piece] if far_own else hop_send.at[index, piece, origin],
             recv_sem=hop_recv.at[index, piece, origin],
-            device_id={"lon": jnp.clip(place + way, 0, count - 1)},
+            device_id={"lon": jnp.clip(place + way * stride, 0, count - 1)},
             device_id_type=MESH,
         )
 
@@ -137,8 +179,11 @@
             device_id_type=MESH,
         )
 
-    def has(way):
-        return place < count - 1 if way > 0 else place > 0
+    def has(way, stride=1):
+        return place < count - stride if way > 0 else place >= stride
+
+    def strides(piece):
+        return (1, 2) if pieces[piece][0] < 2 else (1,)
 
     def has_section(way):
         return section < sections - 1 if way > 0 else section > 0
@@ -146,11 +191,13 @@
     barrier = pltpu.get_barrier_semaphore()
     for way in (1, -1):
 
-        @pl.when(has(way))
-        def _():
-            pl.semaphore_signal(
-                barrier, inc=1, device_id={"lon": place + way}, device_id_type=MESH
-            )
+        for stride in (1, 2):
+
+            @pl.when(has(way, stride))
+            def _():
+                pl.semaphore_signal(
+                    barrier, inc=1, device_id={"lon": place + way * stride}, device_id_type=MESH
+                )
 
         @pl.when(has_section(way))
         def _():
@@ -162,15 +209,17 @@
     pl.semaphore_signal(barrier, inc=1, device_id={"lat": 1 - row_half}, device_id_type=MESH)
     greeted = 2
     for way in (1, -1):
-        greeted = greeted + jnp.where(has(way), 1, 0) + jnp.where(has_section(way), 1, 0)
+        greeted = greeted + jnp.where(has(way), 1, 0) + jnp.where(has(way, 2), 1, 0)
+        greeted = greeted + jnp.where(has_section(way), 1, 0)
     pl.semaphore_wait(barrier, greeted)
 
     def send_own(piece):
         for way in (1, -1):
-
-            @pl.when(has(way))
-            def _():
-                hop(piece, way, place, True).start()
+            for stride in strides(piece):
+
+                @pl.when(has(way, stride))
+                def _():
+                    hop(piece, way, place, True, stride).start()
 
     def term_copy():
         return pltpu.make_async_remote_copy(
@@ -209,42 +258,100 @@
 
                 lax.fori_loop(0, count, arrive, 0)
 
+    tile_rows = tile.shape[0]
+
+    def mate_copy(number, source, target):
+        return pltpu.make_async_remote_copy(
+            src_ref=source,
+            dst_ref=target,
+            send_sem=mate_sem.at[number, 0],
+            recv_sem=mate_sem.at[number, 1],
+            device_id={"lon": mate},
+            device_id_type=MESH,
+        )
+
+    def slot_rows(whose):
+        return pl.ds(pl.multiple_of(whose * tile_rows, TILE_ROWS), tile_rows)
+
+    def tile_slot(whose):
+        return mate_tokens.at[slot_rows(whose)]
+
+    def twin_copy(whose):
+        return pltpu.make_async_remote_copy(
+            src_ref=tile,
+            dst_ref=tokens.at[slot_rows(whose)],
+            send_sem=mate_sem.at[3, 0],
+            recv_sem=mate_sem.at[3, 1],
+            device_id={"lat": 1 - row_half},
+            device_id_type=MESH,
+        )
+
+    def tile_copy():
+        return mate_copy(0, tile, tile_slot(row_half))
+
+    def sum_copy():
+        return mate_copy(1, mate_sent, mate_terms)
+
+    def share_copy(whose):
+        return pltpu.make_async_remote_copy(
+            src_ref=tile_slot(whose),
+            dst_ref=tile_slot(whose),
+            send_sem=mate_sem.at[2, 0],
+            recv_sem=mate_sem.at[2, 1],
+            device_id={"lat": 1 - row_half},
+            device_id_type=MESH,
+        )
+
     def run_up():
-        width = hidden.shape[1] // 4
+        twin_copy(1 - row_half).wait_recv()
+        share_copy(1 - row_half).wait_recv()
+        share_copy(row_half).wait_send()
 
         def block(index, carry):
-            columns = pl.ds(pl.multiple_of(index * width, 128), width)
-            total = jnp.dot(
-                tokens[...], up_whole[0, :, columns], preferred_element_type=jnp.float32
-            )
-            total = total + bias[:, columns]
-            total = 0.5 * total * (1.0 + lax.erf(total * (0.5**0.5)))
-            hidden[:, columns] = total.astype(hidden.dtype)
+            columns = pl.ds(pl.multiple_of(index * BLOCK, 128), BLOCK)
+            biases = bias[:, pl.ds(pl.multiple_of(parity * units + index * BLOCK, 128), BLOCK)]
+            for group, rows in enumerate((mate_tokens, tokens)):
+                total = jnp.dot(
+                    rows[...], up_whole[0, :, columns], preferred_element_type=jnp.float32
+                )
+                total = total + biases
+                total = 0.5 * total * (1.0 + lax.erf(total * (0.5**0.5)))
+                hidden[group, :, columns] = total.astype(hidden.dtype)
             return carry
 
-        lax.fori_loop(0, 4, block, 0)
+        lax.fori_loop(0, units // BLOCK, block, 0)
 
     def run_down():
-        height = own_terms.shape[0]
-        depth, width = shards[1].shape[1:]
+        width = down_whole.shape[2]
 
         def block(whose, result):
-            rows = pl.ds(pl.multiple_of(whose * height, TILE_ROWS), height)
-            for origin in range(count):
-                term = jnp.dot(
-                    hidden[rows, :],
-                    down_whole[0, origin * depth : (origin + 1) * depth, :],
-                    preferred_element_type=jnp.float32,
-                )
-                result[:, origin * width : (origin + 1) * width] = term.astype(result.dtype)
+            rows = pl.ds(pl.multiple_of(whose * tile_rows, TILE_ROWS), tile_rows)
+            for group in range(2):
+                for origin in range(count):
+                    term = jnp.dot(
+                        hidden[group, rows, :],
+                        down_whole[0, origin * units : (origin + 1) * units, :],
+                        preferred_element_type=jnp.float32,
+                    )
+                    result[group, :, origin * width : (origin + 1) * width] = term.astype(
+                        result.dtype
+                    )
 
         block(1 - row_half, sent_terms)
         term_copy().start()
         block(row_half, own_terms)
 
+    def lat_sum(group):
+        return own_terms[group].astype(jnp.float32) + peer_terms[group].astype(jnp.float32)
+
+    def send_mate_sum():
+        term_copy().wait_recv()
+        mate_sent[...] = lat_sum(0).astype(mate_sent.dtype)
+        sum_copy().start()
+
     def finish_mlp():
-        term_copy().wait_recv()
-        total = own_terms[...].astype(jnp.float32) + peer_terms[...].astype(jnp.float32)
+        sum_copy().wait_recv()
+        total = lat_sum(1) + mate_terms[...].astype(jnp.float32)
         moved = tile[...].astype(jnp.float32) + layer_norm(total, gain[...])
         handed[...] = moved.astype(handed.dtype)
 
@@ -254,18 +361,17 @@
 
     own = [
         pltpu.make_async_copy(
-            shards[kind],
+            source_of(kind, 0, extent(kind), parity),
             wholes[kind].at[
-                :,
-                pl.ds(
-                    pl.multiple_of(place * shards[kind].shape[1], TILE_ROWS),
-                    shards[kind].shape[1],
-                ),
+                :, pl.ds(pl.multiple_of(place * extent(kind), TILE_ROWS), extent(kind))
             ],
             own_sem.at[kind],
         )
         for kind in range(kinds)
     ]
+    tile_copy().start()
+    twin_copy(row_half).start()
+    tokens[slot_rows(row_half), :] = tile[...]
     for piece in range(AHEAD):
         send_own(piece)
     for copy in own:
@@ -285,7 +391,12 @@
             await_across(1)
             run_down()
         if piece == DOWN_READY + 1:
+            send_mate_sum()
+        if piece == DOWN_READY + 2:
             finish_mlp()
+        if piece == 1:
+            tile_copy().wait_recv()
+            share_copy(row_half).start()
 
         def step(distance, carry):
             for way in (1, -1):
@@ -293,11 +404,12 @@
 
                 @pl.when((origin >= 0) & (origin < count))
                 def _():
-                    hop(piece, way, origin, False).wait_recv()
-
-                    @pl.when(has(way))
+                    stride = strides(piece)[-1]
+                    hop(piece, way, origin, False, stride).wait_recv()
+
+                    @pl.when(has(way, stride))
                     def _():
-                        hop(piece, way, origin, False).start()
+                        hop(piece, way, origin, False, stride).start()
 
                     across(piece, origin, half).start()
 
@@ -315,14 +427,26 @@
 
             for way in (1, -1):
 
-                @pl.when(has(way) & ((place - origin) * way >= 0))
+                stride = strides(piece)[-1]
+
+                @pl.when(has(way, stride) & ((place - origin) * way > 0))
                 def _():
-                    hop(piece, way, origin, False).wait_send()
+                    hop(piece, way, origin, False, stride).wait_send()
 
             return carry
 
         lax.fori_loop(0, count, drain, 0)
+        for way in (1, -1):
+            for stride in strides(piece):
+
+                @pl.when(has(way, stride))
+                def _():
+                    hop(piece, way, place, True, stride).wait_send()
+
     term_copy().wait_send()
+    tile_copy().wait_send()
+    twin_copy(row_half).wait_send()
+    sum_copy().wait_send()
 
     @pl.when(has_section(1))
     def _():
@@ -337,25 +461,33 @@
         fresh_copy().wait()
 
 
-def relayed(shards, tokens, bias, tile, gain, fresh):
+def relayed(shards, bias, tile, gain, fresh):
     count = lax.axis_size("lon")
     pieces = sum(SPLITS)
     wholes = [
         jax.ShapeDtypeStruct((w.shape[0], count * w.shape[1], w.shape[2]), w.dtype)
         for w in shards
     ]
+    units = shards[0].shape[2] // 2
+    up_shape = wholes[0].shape[:2] + (units,)
+    down_shape = (1, count * units, shards[1].shape[2])
+    pair_shape = (2 * tile.shape[0], tile.shape[1])
     near = pl.BlockSpec(memory_space=pltpu.VMEM)
     far = pl.BlockSpec(memory_space=pl.ANY)
     return pl.pallas_call(
         functools.partial(relay_kernel, count, lax.axis_size("section")),
         out_shape=[jax.ShapeDtypeStruct(tile.shape, tile.dtype)] * 2 + wholes[2:],
-        in_specs=[far] * len(shards) + [near] * 4 + [far],
+        in_specs=[far] * len(shards) + [near] * 3 + [far],
         out_specs=[near, far, far, far],
         scratch_shapes=[
-            pltpu.VMEM(wholes[0].shape, wholes[0].dtype),
-            pltpu.VMEM(wholes[1].shape, wholes[1].dtype),
-            pltpu.VMEM((tokens.shape[0], shards[0].shape[2]), tile.dtype),
-            pltpu.VMEM(tile.shape, tile.dtype),
+            pltpu.VMEM(up_shape, wholes[0].dtype),
+            pltpu.VMEM(down_shape, wholes[1].dtype),
+            pltpu.VMEM((2, pair_shape[0], units), tile.dtype),
+            pltpu.VMEM((2,) + tile.shape, tile.dtype),
+            pltpu.VMEM((2,) + tile.shape, tile.dtype),
+            pltpu.VMEM((2,) + tile.shape, tile.dtype),
+            pltpu.VMEM(pair_shape, tile.dtype),
+            pltpu.VMEM(pair_shape, tile.dtype),
             pltpu.VMEM(tile.shape, tile.dtype),
             pltpu.VMEM(tile.shape, tile.dtype),
             pltpu.SemaphoreType.DMA((2, pieces, count)),
@@ -366,22 +498,24 @@
             pltpu.SemaphoreType.DMA,
             pltpu.SemaphoreType.DMA,
             pltpu.SemaphoreType.DMA((3,)),
+            pltpu.SemaphoreType.DMA((2, pieces)),
+            pltpu.SemaphoreType.DMA((4, 2)),
         ],
         compiler_params=pltpu.CompilerParams(
             collective_id=0, has_side_effects=True, vmem_limit_bytes=VMEM_BYTES
         ),
-    )(*shards, tokens, bias, tile, gain, fresh)
-
-
-def gathered(shards, tokens, bias, tile, gain, fresh):
+    )(*shards, bias, tile, gain, fresh)
+
+
+def gathered(shards, bias, tile, gain, fresh):
+    tokens = lax.all_gather(tile, "lat", axis=0, tiled=True)
     up_whole, down_whole, qkv_whole, out_whole = [
         lax.all_gather(w, "lon", axis=1, tiled=True) for w in shards
     ]
     pre_act = jnp.dot(tokens, up_whole[0], preferred_element_type=jnp.float32)
     hidden = jax.nn.gelu(pre_act + bias, approximate=False).astype(jnp.bfloat16)
     down_terms = times_columns(hidden, down_whole).astype(jnp.bfloat16)
-    mlp_sum = lax.psum_scatter(down_terms, "lat", scatter_dimension=0, tiled=True)
-    handed = tile.astype(jnp.float32) + layer_norm(mlp_sum.astype(jnp.float32), gain)
+    handed = tile.astype(jnp.float32) + layer_norm(summed_over_lat(down_terms), gain)
     handed = handed.astype(jnp.bfloat16)
     passed = shifted(handed, "section", 1)
     entering = jnp.where(lax.axis_index("section") == 0, fresh, passed)
@@ -390,6 +524,8 @@
 
 def mlp_and_weights(shards, *rest):
     fits = all(w.shape[1] % (2 * n * TILE_ROWS) == 0 for w, n in zip(shards, SPLITS))
+    fits = fits and shards[1].shape[1] % (4 * SPLITS[1] * TILE_ROWS) == 0
+    fits = fits and shards[0].shape[2] % (2 * BLOCK) == 0 and lax.axis_size("lon") % 2 == 0
     pairs = lax.axis_size("grp") == 2 and lax.axis_size("lat") == 2
     return relayed(shards, *rest) if fits and pairs else gathered(shards, *rest)
 
@@ -417,10 +553,8 @@
 ):
     tile_in = section_input[0]
     height, breadth, width = tile_in.shape
-    token_rows = lax.all_gather(tile_in, "lat", axis=0, tiled=True).reshape(-1, width)
     handed, entering, qkv_whole, out_whole = mlp_and_weights(
         [up_weight, down_weight, jnp.swapaxes(qkv_weight[0], 0, 1), out_weight],
-        token_rows,
         up_bias,
         tile_in.reshape(-1, width),
         mlp_gain,
@@ -435,12 +569,13 @@
     rolled = lax.dynamic_slice_in_dim(
         jnp.concatenate([entering, after_strip], 1), shift_lon, breadth, 1
     )
-    region_marks = regions.astype(jnp.bfloat16)
-    grid, grid_marks = (
-        lax.all_gather(rolled, "lat", axis=0, tiled=True),
-        lax.all_gather(region_marks, "lat", axis=0, tiled=True),
-    )
-    grid = jnp.roll(grid, -shift_lat, axis=0)
+    grid = lax.all_gather(rolled, "lat", axis=0, tiled=True)
+    all_columns = breadth * lax.axis_size("lon")
+    own_columns = lax.axis_index("lon") * breadth + jnp.arange(breadth)
+    row_slabs = slab_ids(jnp.arange(grid.shape[0]), grid.shape[0], shift_lat)
+    column_slabs = slab_ids(own_columns, all_columns, shift_lon)
+    grid_marks = 3 * row_slabs[:, None] + column_slabs[None, :]
+    grid = turned(grid, shift_lat)
     grid_height = grid.shape[0]
     flat_grid = grid.reshape(-1, width)
     heads_local = logit_scale.shape[1]
@@ -452,12 +587,9 @@
         grid_height * breadth, heads_local * head_size
     )
     out_terms = times_columns(context, out_whole)
-    out_terms = jnp.roll(out_terms.reshape(grid_height, breadth, width), shift_lat, axis=0).reshape(
-        -1, width
-    )
-    attn_sum = lax.psum_scatter(
-        out_terms.astype(jnp.bfloat16), "lat", scatter_dimension=0, tiled=True
-    ).astype(jnp.float32)
+    out_terms = out_terms.astype(jnp.bfloat16).reshape(grid_height, breadth, width)
+    out_terms = turned(out_terms, grid_height - shift_lat).reshape(-1, width)
+    attn_sum = summed_over_lat(out_terms)
     branch = layer_norm(attn_sum, attn_gain[0]).astype(jnp.bfloat16).reshape(height, breadth, width)
     tail_strip = from_behind(branch[:, -strip_width:], "lon", 1)
     branch = lax.dynamic_slice_in_dim(

time: 221 us -> 161 us (0.73)
  Pallas kernels: 149 us -> 123 us
  between operations: 20 us -> 8.07 us
  local copies, waits for them, and re-layouts: 13.8 us -> 6.03 us
  blocking collectives: 6.93 us -> 2.37 us
  other arithmetic: 7.57 us -> 3.08 us
  waiting for transfers between devices: 11.6 us -> 8.88 us
    pallas_call x1, Pallas kernels: 149 us -> 123 us  [relayed(): pl.pallas_call(functools.partial(relay_kernel, count, lax.axis_size('sect...]
    unnamed x29 -> x13, local copies, waits for them, and re-layouts: 9.28 us -> 0.89 us
    reduce_scatter x1 -> x0, waiting for transfers between devices: 5.67 us -> none  [per_device(): lax.psum_scatter(out_terms.astype(jnp.bfloat16), 'lat', scatter_dimension...]
    all_gather x3 -> x1, blocking collectives: 6.93 us -> 2.37 us  [per_device(): grid = lax.all_gather(rolled, 'lat', axis=0, tiled=True)]
    ppermute x2 -> x3, waiting for transfers between devices: 5.96 us -> 8.88 us  [from_behind(): return lax.ppermute(block, axis, route)]
  transfers between devices with their start and end apart: 3 -> 3, of which waited for: 2 -> 2; matrix products, arithmetic and copies ran while one was open for 1% -> 2% of each run, Pallas kernels for 0% -> 0%
where the time goes in v3:
time: 161 us
  Pallas kernels  123 us (76%)
  waiting for transfers between devices  8.88 us (6%)
  between operations  8.07 us (5%)
  matrix products  6.92 us (4%)
  local copies, waits for them, and re-layouts  6.03 us (4%)
  other arithmetic  3.08 us (2%)
  starting transfers between devices  2.66 us (2%)
  blocking collectives  2.37 us (1%)
    pallas_call x1, Pallas kernels, relayed(): pl.pallas_call(functools.partial(relay_kernel, count, lax.axis_size('sect...  123 us
    ppermute x3, waiting for transfers between devices, from_behind(): return lax.ppermute(block, axis, route)  8.88 us
    dot_general x1, matrix products, per_device(): jnp.einsum('td,kdc->ktc', flat_grid, qkv_whole, preferred_element_type=jn...  3.33 us
  transfers between devices with their start and end apart: 3, of which 2 were waited for; matrix products, arithmetic and copies ran while one was open for 2% of the time, Pallas kernels for 0%

profile of v3, /device:TPU:0, one launch (start us, length us, event | category | flops | bytes accessed | tf_op | source)
XLA Modules:
  0.0 160.6 jit_solution(1410705611625738816)
XLA Ops:
  0.7 122.5 %shard_map.131 = (bf16[128,1536]{1,0:T(8,128)(2,1)}, bf16[128,1536]{1,0:T(8,128)(2,1)}, bf16[3,1536,384]{2,1,0:T(8,128)(2,1)}, bf16[1,1536,384]{2,1,0:T(8,128)(2,1)}) custom-call(bf16[1,384,1536]{2,1,0:T(8,128)(2,1)} %refs_0_.1, bf16[1,1536,384]{2,1,0:T(8,128)(2,1)} %refs_1_.1, bf16[3,384,384]{2,1,0:T(8,128)(2,1)} %bitcast.53, bf16[1,384,384]{2,1,0:T(8,128)(2,1)} %refs_3_.1, ...), custom_call_target="tpu_custom_call" | custom-call | tf_op jit(solution)/shard_map/pallas_call | solution.py:477
  123.2 1.1 slice.31
  124.3 2.4 %collective-permute-start = (bf16[16,4,1536]{2,1,0:T(4,128)(2,1)S(1)}, bf16[16,4,1536]{2,1,0:T(4,128)(2,1)S(1)}, u32[]{:S(2)}, u32[]{:S(2)}) collective-permute-start(bf16[16,4,1536]{2,1,0:T(4,128)(2,1)S(1)} %slice.31), channel_id=1, source_target_pairs={{1,0},{2,1},{3,2},{0,3},{5,4},{6,5},{7,6},{4,7},{9,8},{10,9},{11,1... | collective-permute-start | bytes 589832 | tf_op jit(solution)/shard_map/ppermute | solution.py:22
  126.7 0.6 fusion.31
  131.6 1.7 %copy.37 = bf16[4,384,384]{1,2,0:T(8,128)(2,1)S(1)} copy(bf16[4,384,384]{2,1,0:T(8,128)(2,1)} %bitcast.52) | data formatting | bytes 2359296 | tf_op jit(solution)/shard_map/reshape | solution.py:534
  135.4 0.3 fusion.18
  135.8 2.4 %all_gather.3 = bf16[32,8,1536]{2,1,0:T(8,128)(2,1)S(1)} all-gather(bf16[16,8,1536]{2,1,0:T(8,128)(2,1)S(1)} %fusion.18), channel_id=1, replica_groups=mesh['grp'=2,'section'=2,'lat'=2,'lon'=4] {'lat'}, dimensions={0}, use_global_device_ids=true | all-gather | bytes 1179648 | tf_op jit(solution)/shard_map/all_gather | solution.py:572
  138.1 3.3 %fusion.6 = bf16[3,256,384]{1,2,0:T(8,128)(2,1)S(1)} fusion(bf16[3,1536,384]{2,1,0:T(8,128)(2,1)} %get-tuple-element.8, s32[]{:T(128)S(6)} %select_n.23, bf16[32,8,1536]{2,1,0:T(8,128)(2,1)S(1)} %all_gather.3), kind=kOutput, calls=%fused_computation.13 | convolution fusion | flops 906657792 | bytes 4915204 | tf_op jit(solution)/shard_map/td,kdc->ktc/dot_general | solution.py:583
  141.5 0.2 reshape_transpose_reshape_squeeze.10
  141.7 0.3 multiply_reduce_fusion.2
  142.0 0.2 reshape_transpose_reshape_squeeze.11
  142.2 0.3 multiply_reduce_fusion.1
  142.5 0.2 reshape_transpose_reshape_squeeze.9
  142.8 1.3 fusion.5
  144.1 1.7 %fusion.7 = bf16[4,64,6,64]{1,3,2,0:T(8,128)(2,1)S(1)} fusion(f32[4,6,64,64]{2,3,1,0:T(8,128)} %fusion.5, bf16[4,64,6,64]{1,0,3,2:T(4,128)(2,1)S(1)} %reshape_transpose_reshape_squeeze.9), kind=kOutput, calls=%fused_computation.15 | convolution fusion | flops 12879423 | bytes 786432 | tf_op jit(solution)/shard_map/whij,wjhd->wihd/dot_general | solution.py:82
  145.8 0.3 copy.36
  146.1 0.3 reshape_reshape_transpose_reshape.3
  146.4 0.6 fusion
  147.0 0.3 fusion.9
  147.7 1.4 collective-permute-done.1
  149.3 0.3 multiply_reduce_fusion
  151.3 7.4 %collective-permute-done.2 = bf16[16,4,1536]{2,1,0:T(4,128)(2,1)S(1)} collective-permute-done((bf16[16,4,1536]{2,1,0:T(4,128)(2,1)S(1)}, bf16[16,4,1536]{2,1,0:T(4,128)(2,1)S(1)}, u32[]{:S(2)}, u32[]{:S(2)}) %collective-permute-start.2) | collective-permute-done | bytes 196640 | tf_op jit(solution)/shard_map/ppermute | solution.py:22
  158.7 1.1 fusion.16
  159.8 0.7 copy.47
  (36 shorter events, 1.5 us)
Async XLA Ops:
  0.6 126.1 %copy-start.4 = (s32[2]{0:T(128)S(1)}, s32[2]{0:T(128)}, u32[]{:S(2)}) copy-start(s32[2]{0:T(128)} %param.15) | copy-start | bytes 28
  0.6 130.8 %copy-start.2 = (f32[1,6,64,64]{3,2,1,0:T(8,128)S(1)}, f32[1,6,64,64]{3,2,1,0:T(8,128)}, u32[]{:S(2)}) copy-start(f32[1,6,64,64]{3,2,1,0:T(8,128)} %param.22) | copy-start | bytes 294916
  123.2 12.2 %copy-start = (bf16[128,1536]{1,0:T(8,128)(2,1)S(1)}, bf16[128,1536]{1,0:T(8,128)(2,1)}, u32[]{:S(2)}) copy-start(bf16[128,1536]{1,0:T(8,128)(2,1)} %get-tuple-element.7) | copy-start | bytes 1179652
  124.3 11.1 %collective-permute-start = (bf16[16,4,1536]{2,1,0:T(4,128)(2,1)S(1)}, bf16[16,4,1536]{2,1,0:T(4,128)(2,1)S(1)}, u32[]{:S(2)}, u32[]{:S(2)}) collective-permute-start(bf16[16,4,1536]{2,1,0:T(4,128)(2,1)S(1)} %slice.31), channel_id=1, source_target_pairs={{1,0},{2,1},{3,2},{0,3},{5,4},{6,5},{7,6},{4,7},{9,8},{10,9},{11,1... | collective-permute-start | bytes 589832 | tf_op jit(solution)/shard_map/ppermute | solution.py:22
  141.5 1.2 copy-start.5
  147.0 0.7 copy-start.3
  147.4 1.8 %collective-permute-start.1 = (bf16[128,1536]{1,0:T(8,128)(2,1)S(1)}, bf16[128,1536]{1,0:T(8,128)(2,1)S(1)}, u32[]{:S(2)}, u32[]{:S(2)}) collective-permute-start(bf16[128,1536]{1,0:T(8,128)(2,1)S(1)} %constant_dynamic-slice_fusion), channel_id=1, source_target_pairs={{4,0},{0,4},{5,1},{1,5},{6,2},{2,6},{7,3},{3,7},{12,8},{8,12},{13,... | collective-permute-start | bytes 1179656 | tf_op jit(solution)/shard_map/ppermute | solution.py:22
  149.6 10.2 %copy-start.1 = (bf16[128,1536]{1,0:T(8,128)(2,1)S(1)}, bf16[128,1536]{1,0:T(8,128)(2,1)}, u32[]{:S(2)}) copy-start(bf16[128,1536]{1,0:T(8,128)(2,1)} %get-tuple-element.6) | copy-start | bytes 1179652
  149.9 8.8 %collective-permute-start.2 = (bf16[16,4,1536]{2,1,0:T(4,128)(2,1)S(1)}, bf16[16,4,1536]{2,1,0:T(4,128)(2,1)S(1)}, u32[]{:S(2)}, u32[]{:S(2)}) collective-permute-start(bf16[16,4,1536]{2,1,0:T(4,128)(2,1)S(1)} %slice.35), channel_id=1, source_target_pairs={{3,0},{0,1},{1,2},{2,3},{7,4},{4,5},{5,6},{6,7},{11,8},{8,9},{9,10... | collective-permute-start | bytes 589832 | tf_op jit(solution)/shard_map/ppermute | solution.py:22
